TPU v7x, 768 devices: a whole 4x8x12 slice. The times are simulated.
768 devices in a mesh: grp: 2 (over x_hi), seq: 12 (over z), tp: 32 (over x_lo, y, core).
Axes of the slice: x: 4 (x_hi: 2, x_lo: 2; x = x_hi * 2 + x_lo), y: 8, z: 12, core: 2. Of those that a mesh axis runs over, the one named last changes fastest.
Arguments:
- queries: bfloat16 [2, 73728, 1792], P('grp', ('seq', 'tp')), may hold values from -40 to 40
- keys: bfloat16 [2, 73728, 256], P('grp', ('seq', 'tp')), may hold values from -40 to 40
- values: bfloat16 [2, 73728, 256], P('grp', ('seq', 'tp')), may hold values from -6 to 6
- grad_out: bfloat16 [2, 73728, 1792], P('grp', ('seq', 'tp')), may hold values from -6 to 6
- slot_pos: int32 [2, 73728], P('grp', ('seq', 'tp')), may hold values from -1 to 129023, as said below
- counts: int32 [2, 384], P('grp', ('seq', 'tp')), may hold values from 144 to 192, as said below
- seg_id: int32 [129024], P(('seq', 'tp')), may hold values from 0 to 306, as said below
Outputs:
- attended: bfloat16 [2, 73728, 1792], P('grp', ('seq', 'tp'))
- grad_queries: bfloat16 [2, 73728, 1792], P('grp', ('seq', 'tp'))
- key_gradients: bfloat16 [2, 73728, 256], P('grp', ('seq', 'tp'))
- value_gradients: bfloat16 [2, 73728, 256], P('grp', ('seq', 'tp'))
Inputs may be any that keep to these rules, and one draw needn't show every extreme that they name: Each position block holds 336 positions, and its und and gen counts add up to 336; some block has exactly 192 understanding tokens and some other exactly 192 generation tokens. `slot_pos`: the live slots of a modality in block b hold, in increasing order, that modality's positions among b * 336 to (b + 1) * 336 - 1; every position is held by exactly one live slot; the slots after the live ones hold -1. `seg_id`: segment ids start at 0 and rise by one from segment to segment; a segment covers 1 to 673 consecutive positions, and one covers exactly 673; the number of segments is fixed by the sizes.
All inputs are finite; a program needn't handle non-finite values.
Results may differ from a plain program's by a relative error of at most 0.03.
Values may be sent and summed in bfloat16 or wider, within the bound.
No kernel may reach another device: no remote copies, remote signals or barrier semaphores. Data moves between devices by JAX's collectives and lax.ppermute only.
A program may use at most 64 MiB of HBM per device.

v0:
```python
import jax
import jax.numpy as jnp
from jax import lax
from jax.sharding import PartitionSpec as P

HEAD_SIZE = 128
KEY_BLOCK_SPAN = 3


def partner(block, axis, distance):
    count = lax.axis_size(axis)
    route = []
    for low in range(count):
        high = low | 1 << distance
        if high != low and high < count:
            route += [(low, high), (high, low)]
    return lax.ppermute(block, axis, route)


def shortened(value):
    return jax.tree.map(lambda a: a.astype(jnp.bfloat16) if a.dtype == jnp.float32 else a, value)


def from_behind(block, axis, distance):
    devices = range(lax.axis_size(axis))
    route = [(i - distance, i) for i in devices if i - distance in devices]
    return lax.ppermute(block, axis, route)


def head_forward(qh, kh, vh, mask, live, scale):
    scores = jnp.einsum("qgd,kd->gqk", qh, kh, preferred_element_type=jnp.float32) * scale
    scores = jnp.where(mask[None], scores, -jnp.inf)
    top = jnp.max(scores, axis=-1)
    top = jnp.where(live[None], top, 0.0)
    expo = jnp.exp(scores - top[..., None])
    total = jnp.sum(expo, axis=-1)
    total = jnp.where(live[None], total, 1.0)
    weights = (expo / total[..., None]).astype(jnp.bfloat16)
    result = jnp.einsum("gqk,kd->qgd", weights, vh, preferred_element_type=jnp.float32)
    result = jnp.where(live[:, None, None], result, 0.0).astype(jnp.bfloat16)
    lse = top + jnp.log(total)
    prob = jnp.exp(jnp.where(mask[None], scores - lse[..., None], -jnp.inf))
    return (result, prob)


def head_backward(qh, kh, vh, oh, dh, prob, scale):
    delta = jnp.transpose(jnp.sum(oh.astype(jnp.float32) * dh.astype(jnp.float32), axis=-1))
    dprob = jnp.einsum("qgd,kd->gqk", dh, vh, preferred_element_type=jnp.float32)
    dscore = (prob * (dprob - delta[..., None]) * scale).astype(jnp.bfloat16)
    grad_q = jnp.einsum("gqk,kd->qgd", dscore, kh, preferred_element_type=jnp.float32)
    grad_k = jnp.einsum("gqk,qgd->kd", dscore, qh, preferred_element_type=jnp.float32)
    grad_v = jnp.einsum(
        "gqk,qgd->kd", prob.astype(jnp.bfloat16), dh, preferred_element_type=jnp.float32
    )
    return (grad_q, grad_k, grad_v)


def drop_missing(moved, block, distance):
    key_part, val_part, pos_part, seg_part = moved
    return (key_part, val_part, pos_part, jnp.where(block >= distance, seg_part, -1))


def join_all(pieces):
    return tuple((jnp.concatenate([piece[member] for piece in pieces], 0) for member in range(4)))


def body(queries, keys, values, grad_out, slot_pos, counts, seg_id):
    scale = 1.0 / HEAD_SIZE**0.5
    q_local = queries[0]
    d_local = grad_out[0]
    tok = q_local.shape[0]
    kv_heads = keys.shape[2] // HEAD_SIZE
    sharing = q_local.shape[1] // (kv_heads * HEAD_SIZE)
    window_width = seg_id.shape[0]
    block = lax.axis_index(("seq", "tp"))
    live = jnp.arange(tok) < counts[0, 0]
    pos = slot_pos[0]
    local = pos - block * window_width
    onehot = local[:, None] == jnp.arange(window_width)[None, :]
    seg = jnp.where(live, jnp.sum(jnp.where(onehot, seg_id[None, :], 0), axis=1), -1)
    own = (keys[0], values[0], pos, seg)
    other = partner((own[0], own[1], own[2], own[3]), "grp", 0)
    pair = join_all([own, other])
    windows = [pair]
    for distance in range(1, KEY_BLOCK_SPAN):
        moved = jax.tree.map(
            lambda part, own: part.astype(own.dtype),
            from_behind(shortened(pair), ("seq", "tp"), distance),
            pair,
        )
        windows.append(drop_missing(moved, block, distance))
    key_w, val_w, pos_w, seg_w = join_all(windows)
    mask = (
        live[:, None]
        & (seg_w[None, :] == seg[:, None])
        & (seg_w[None, :] >= 0)
        & (pos_w[None, :] <= pos[:, None])
    )
    q_heads = q_local.reshape(tok, kv_heads, sharing, HEAD_SIZE)
    d_heads = d_local.reshape(tok, kv_heads, sharing, HEAD_SIZE)
    out_list, dq_list, dk_list, dv_list = ([], [], [], [])
    for head_number in range(kv_heads):
        kh = key_w[:, head_number * HEAD_SIZE : (head_number + 1) * HEAD_SIZE]
        vh = val_w[:, head_number * HEAD_SIZE : (head_number + 1) * HEAD_SIZE]
        oh, prob = head_forward(q_heads[:, head_number], kh, vh, mask, live, scale)
        gq, gk, gv = head_backward(
            q_heads[:, head_number], kh, vh, oh, d_heads[:, head_number], prob, scale
        )
        out_list.append(oh)
        dq_list.append(gq.astype(jnp.bfloat16))
        dk_list.append(gk)
        dv_list.append(gv)
    attended = jnp.stack(out_list, axis=1).reshape(tok, -1)
    grad_queries = jnp.stack(dq_list, axis=1).reshape(tok, -1)
    dk_window = jnp.concatenate(dk_list, axis=1)
    dv_window = jnp.concatenate(dv_list, axis=1)
    span = 2 * tok
    total_k = dk_window[:span]
    total_v = dv_window[:span]
    for distance in range(1, KEY_BLOCK_SPAN):
        piece = (
            dk_window[distance * span : (distance + 1) * span],
            dv_window[distance * span : (distance + 1) * span],
        )
        back = from_behind((piece[0], piece[1]), ("seq", "tp"), -distance)
        total_k = total_k + back[0]
        total_v = total_v + back[1]
    returned = partner((total_k[tok:], total_v[tok:]), "grp", 0)
    grad_k = total_k[:tok] + returned[0]
    grad_v = total_v[:tok] + returned[1]
    return (
        attended[None],
        grad_queries[None],
        grad_k.astype(jnp.bfloat16)[None],
        grad_v.astype(jnp.bfloat16)[None],
    )


def solution(mesh):
    return jax.shard_map(
        body,
        mesh=mesh,
        in_specs=(
            P("grp", ("seq", "tp"), None),
            P("grp", ("seq", "tp"), None),
            P("grp", ("seq", "tp"), None),
            P("grp", ("seq", "tp"), None),
            P("grp", ("seq", "tp")),
            P("grp", ("seq", "tp")),
            P(("seq", "tp")),
        ),
        out_specs=(
            P("grp", ("seq", "tp"), None),
            P("grp", ("seq", "tp"), None),
            P("grp", ("seq", "tp"), None),
            P("grp", ("seq", "tp"), None),
        ),
        check_vma=False,
    )
```

profile of v0, /device:TPU:249, one launch (start us, length us, event | category | flops | bytes accessed | tf_op | source)
XLA Modules:
  0.0 121.2 jit_solution(10960851759793185268)
XLA Ops:
  0.7 4.8 %collective-permute-start.6 = (s32[192]{0:T(256)}, s32[192]{0:T(256)S(1)}, u32[]{:S(2)}, u32[]{:S(2)}) collective-permute-start(s32[192]{0:T(256)} %bitcast.116), channel_id=1, source_target_pairs={{0,384},{384,0},{1,385},{385,1},{2,386},{386,2},{3,387},{387,3},{4... | collective-permute-start | bytes 2312 | tf_op jit(solution)/shard_map/ppermute | solution.py:17
  7.7 2.1 %collective-permute-start.3 = (s32[192]{0:T(256)S(1)}, s32[192]{0:T(256)S(1)}, u32[]{:S(2)}, u32[]{:S(2)}) collective-permute-start(s32[192]{0:T(256)S(1)} %broadcast_select_fusion.6), channel_id=1, source_target_pairs={{0,384},{384,0},{1,385},{385,1},{2,386},{386,2},{3,387},{387,3},{4... | collective-permute-start | bytes 2312 | tf_op jit(solution)/shard_map/ppermute | solution.py:17
  9.9 4.7 %collective-permute-start.9 = (bf16[192,256]{1,0:T(8,128)(2,1)}, bf16[192,256]{1,0:T(8,128)(2,1)S(1)}, u32[]{:S(2)}, u32[]{:S(2)}) collective-permute-start(bf16[192,256]{1,0:T(8,128)(2,1)} %bitcast.108), channel_id=1, source_target_pairs={{0,384},{384,0},{1,385},{385,1},{2,386},{386,2},{3,387},{387,3},{4... | collective-permute-start | bytes 294920 | tf_op jit(solution)/shard_map/ppermute | solution.py:17
  14.5 2.1 %collective-permute-start = (bf16[192,256]{1,0:T(8,128)(2,1)}, bf16[192,256]{1,0:T(8,128)(2,1)S(1)}, u32[]{:S(2)}, u32[]{:S(2)}) collective-permute-start(bf16[192,256]{1,0:T(8,128)(2,1)} %bitcast.111), channel_id=1, source_target_pairs={{0,384},{384,0},{1,385},{385,1},{2,386},{386,2},{3,387},{387,3},{4... | collective-permute-start | bytes 294920 | tf_op jit(solution)/shard_map/ppermute | solution.py:17
  21.4 2.3 %collective-permute-start.5 = (s32[384]{0:T(512)S(1)}, s32[384]{0:T(512)S(1)}, u32[]{:S(2)}, u32[]{:S(2)}) collective-permute-start(s32[384]{0:T(512)S(1)} %pad_add_fusion), channel_id=1, source_target_pairs={{0,2},{1,3},{2,4},{3,5},{4,6},{5,7},{6,8},{7,9},{8,10},{9,11},{10,... | collective-permute-start | bytes 4616 | tf_op jit(solution)/shard_map/ppermute | solution.py:27
  23.8 5.2 %collective-permute-start.4 = (s32[384]{0:T(512)S(1)}, s32[384]{0:T(512)S(1)}, u32[]{:S(2)}, u32[]{:S(2)}) collective-permute-start(s32[384]{0:T(512)S(1)} %pad_add_fusion), channel_id=1, source_target_pairs={{0,1},{1,2},{2,3},{3,4},{4,5},{5,6},{6,7},{7,8},{8,9},{9,10},{10,1... | collective-permute-start | bytes 4616 | tf_op jit(solution)/shard_map/ppermute | solution.py:27
  29.7 1.9 %collective-permute-start.7 = (s32[384]{0:T(512)S(1)}, s32[384]{0:T(512)S(1)}, u32[]{:S(2)}, u32[]{:S(2)}) collective-permute-start(s32[384]{0:T(512)S(1)} %pad_add_fusion.1), channel_id=1, source_target_pairs={{0,1},{1,2},{2,3},{3,4},{4,5},{5,6},{6,7},{7,8},{8,9},{9,10},{10,1... | collective-permute-start | bytes 4616 | tf_op jit(solution)/shard_map/ppermute | solution.py:27
  31.6 3.2 %collective-permute-start.8 = (s32[384]{0:T(512)S(1)}, s32[384]{0:T(512)S(1)}, u32[]{:S(2)}, u32[]{:S(2)}) collective-permute-start(s32[384]{0:T(512)S(1)} %pad_add_fusion.1), channel_id=1, source_target_pairs={{0,2},{1,3},{2,4},{3,5},{4,6},{5,7},{6,8},{7,9},{8,10},{9,11},{10,... | collective-permute-start | bytes 4616 | tf_op jit(solution)/shard_map/ppermute | solution.py:27
  36.7 6.8 %collective-permute-start.10 = (bf16[384,256]{1,0:T(8,128)(2,1)S(1)}, bf16[384,256]{1,0:T(8,128)(2,1)S(1)}, u32[]{:S(2)}, u32[]{:S(2)}) collective-permute-start(bf16[384,256]{1,0:T(8,128)(2,1)S(1)} %pad_maximum_fusion.7), channel_id=1, source_target_pairs={{0,1},{1,2},{2,3},{3,4},{4,5},{5,6},{6,7},{7,8},{8,9},{9,10},{10,1... | collective-permute-start | bytes 589832 | tf_op jit(solution)/shard_map/ppermute | solution.py:27
  43.6 1.9 %collective-permute-start.11 = (bf16[384,256]{1,0:T(8,128)(2,1)S(1)}, bf16[384,256]{1,0:T(8,128)(2,1)S(1)}, u32[]{:S(2)}, u32[]{:S(2)}) collective-permute-start(bf16[384,256]{1,0:T(8,128)(2,1)S(1)} %pad_maximum_fusion.7), channel_id=1, source_target_pairs={{0,2},{1,3},{2,4},{3,5},{4,6},{5,7},{6,8},{7,9},{8,10},{9,11},{10,... | collective-permute-start | bytes 589832 | tf_op jit(solution)/shard_map/ppermute | solution.py:27
  45.9 1.9 %collective-permute-start.1 = (bf16[384,256]{1,0:T(8,128)(2,1)S(1)}, bf16[384,256]{1,0:T(8,128)(2,1)S(1)}, u32[]{:S(2)}, u32[]{:S(2)}) collective-permute-start(bf16[384,256]{1,0:T(8,128)(2,1)S(1)} %pad_maximum_fusion.6), channel_id=1, source_target_pairs={{0,1},{1,2},{2,3},{3,4},{4,5},{5,6},{6,7},{7,8},{8,9},{9,10},{10,1... | collective-permute-start | bytes 589832 | tf_op jit(solution)/shard_map/ppermute | solution.py:27
  47.9 3.9 %collective-permute-start.2 = (bf16[384,256]{1,0:T(8,128)(2,1)S(1)}, bf16[384,256]{1,0:T(8,128)(2,1)S(1)}, u32[]{:S(2)}, u32[]{:S(2)}) collective-permute-start(bf16[384,256]{1,0:T(8,128)(2,1)S(1)} %pad_maximum_fusion.6), channel_id=1, source_target_pairs={{0,2},{1,3},{2,4},{3,5},{4,6},{5,7},{6,8},{7,9},{8,10},{9,11},{10,... | collective-permute-start | bytes 589832 | tf_op jit(solution)/shard_map/ppermute | solution.py:27
  57.7 2.2 %multiply_reduce_fusion.1 = (f32[192,7]{0,1:T(8,128)S(1)}, bf16[128,7,192]{0,2,1:T(8,128)(2,1)}) fusion(bf16[192,1,7,128]{3,2,1,0:T(8,128)(2,1)S(1)} %get-tuple-element.24, f32[7,192,1152]{2,1,0:T(8,128)S(1)} %get-tuple-element.30, f32[7,192]{1,0:T(8,128)S(1)} %get-tuple-element.17, f32[7,192]{1,0:T(8,128)S(1)} %broadcast_select_fusion.3, ...), kind=kOutput, calls=%fused_computation.54 | convolution fusion | flops 402037440 | bytes 7247616 | tf_op jit(solution)/shard_map/gqk,kd->qgd/dot_general | solution.py:39
  59.9 2.3 %fusion.5 = bf16[7,192,1152]{2,1,0:T(8,128)(2,1)S(1)} fusion(f32[7,192,1152]{2,1,0:T(8,128)S(1)} %get-tuple-element.30, f32[7,192]{1,0:T(8,128)S(1)} %bitcast.122, f32[7,192]{1,0:T(8,128)S(1)} %get-tuple-element.16, pred[192,1152]{1,0:T(8,128)(4,1)S(1)} %compare_and_fusion, bf16[1152,256]{1,0:T(8,128)(2,1)S(1)} %pad_maximum_fusion.2, ...), kind=kOutput, calls=%fused_computation.7 | convolution fusion | flops 405651456 | bytes 10215424 | tf_op jit(solution)/shard_map/qgd,kd->gqk/dot_general | solution.py:48
  67.9 2.4 %collective-permute-start.15 = (f32[384,256]{0,1:T(8,128)}, f32[384,256]{0,1:T(8,128)}, u32[]{:S(2)}, u32[]{:S(2)}) collective-permute-start(f32[384,256]{0,1:T(8,128)} %get-tuple-element.20), channel_id=1, source_target_pairs={{1,0},{2,1},{3,2},{4,3},{5,4},{6,5},{7,6},{8,7},{9,8},{10,9},{11,1... | collective-permute-start | bytes 1179656 | tf_op jit(solution)/shard_map/ppermute | solution.py:27
  70.3 2.5 %collective-permute-start.16 = (f32[384,256]{0,1:T(8,128)}, f32[384,256]{0,1:T(8,128)}, u32[]{:S(2)}, u32[]{:S(2)}) collective-permute-start(f32[384,256]{0,1:T(8,128)} %get-tuple-element.21), channel_id=1, source_target_pairs={{2,0},{3,1},{4,2},{5,3},{6,4},{7,5},{8,6},{9,7},{10,8},{11,9},{12,... | collective-permute-start | bytes 1179656 | tf_op jit(solution)/shard_map/ppermute | solution.py:27
  72.8 2.2 %multiply_reduce_fusion = (f32[192,7]{0,1:T(8,128)S(1)}, bf16[128,7,192]{0,2,1:T(8,128)(2,1)}) fusion(bf16[192,1,7,128]{3,2,1,0:T(8,128)(2,1)S(1)} %copy-done.2, f32[7,192,1152]{2,1,0:T(8,128)S(1)} %get-tuple-element.32, f32[7,192]{1,0:T(8,128)S(1)} %get-tuple-element.19, f32[7,192]{1,0:T(8,128)S(1)} %get-tuple-element.28, ...), kind=kOutput, calls=%fused_computation.53 | convolution fusion | flops 402037440 | bytes 7247616 | tf_op jit(solution)/shard_map/gqk,kd->qgd/dot_general | solution.py:39
  75.0 2.4 %fusion.2 = bf16[7,192,1152]{2,1,0:T(8,128)(2,1)S(1)} fusion(f32[7,192,1152]{2,1,0:T(8,128)S(1)} %get-tuple-element.32, f32[7,192]{1,0:T(8,128)S(1)} %bitcast.121, f32[7,192]{1,0:T(8,128)S(1)} %get-tuple-element.18, pred[192,1152]{1,0:T(8,128)(4,1)S(1)} %compare_and_fusion, bf16[1152,256]{1,0:T(8,128)(2,1)S(1)} %pad_maximum_fusion.2, ...), kind=kOutput, calls=%fused_computation.3 | convolution fusion | flops 405651456 | bytes 10215424 | tf_op jit(solution)/shard_map/qgd,kd->gqk/dot_general | solution.py:48
  80.0 2.7 %collective-permute-start.12 = (f32[384,256]{0,1:T(8,128)}, f32[384,256]{0,1:T(8,128)S(1)}, u32[]{:S(2)}, u32[]{:S(2)}) collective-permute-start(f32[384,256]{0,1:T(8,128)} %get-tuple-element.22), channel_id=1, source_target_pairs={{1,0},{2,1},{3,2},{4,3},{5,4},{6,5},{7,6},{8,7},{9,8},{10,9},{11,1... | collective-permute-start | bytes 1179656 | tf_op jit(solution)/shard_map/ppermute | solution.py:27
  82.7 3.1 %collective-permute-start.13 = (f32[384,256]{0,1:T(8,128)}, f32[384,256]{0,1:T(8,128)}, u32[]{:S(2)}, u32[]{:S(2)}) collective-permute-start(f32[384,256]{0,1:T(8,128)} %get-tuple-element.23), channel_id=1, source_target_pairs={{2,0},{3,1},{4,2},{5,3},{6,4},{7,5},{8,6},{9,7},{10,8},{11,9},{12,... | collective-permute-start | bytes 1179656 | tf_op jit(solution)/shard_map/ppermute | solution.py:27
  92.5 4.7 %collective-permute-start.17 = (f32[192,256]{0,1:T(8,128)S(1)}, f32[192,256]{0,1:T(8,128)S(1)}, u32[]{:S(2)}, u32[]{:S(2)}) collective-permute-start(f32[192,256]{0,1:T(8,128)S(1)} %slice.93), channel_id=1, source_target_pairs={{0,384},{384,0},{1,385},{385,1},{2,386},{386,2},{3,387},{387,3},{4... | collective-permute-start | bytes 589832 | tf_op jit(solution)/shard_map/ppermute | solution.py:17
  99.4 4.4 %collective-permute-start.14 = (f32[192,256]{0,1:T(8,128)S(1)}, f32[192,256]{0,1:T(8,128)S(1)}, u32[]{:S(2)}, u32[]{:S(2)}) collective-permute-start(f32[192,256]{0,1:T(8,128)S(1)} %slice.87), channel_id=1, source_target_pairs={{0,384},{384,0},{1,385},{385,1},{2,386},{386,2},{3,387},{387,3},{4... | collective-permute-start | bytes 589832 | tf_op jit(solution)/shard_map/ppermute | solution.py:17
  103.8 11.0 %collective-permute-done.17 = f32[192,256]{0,1:T(8,128)S(1)} collective-permute-done((f32[192,256]{0,1:T(8,128)S(1)}, f32[192,256]{0,1:T(8,128)S(1)}, u32[]{:S(2)}, u32[]{:S(2)}) %collective-permute-start.17) | collective-permute-done | bytes 196640 | tf_op jit(solution)/shard_map/ppermute | solution.py:17
  115.6 4.8 %collective-permute-done.14 = f32[192,256]{0,1:T(8,128)S(1)} collective-permute-done((f32[192,256]{0,1:T(8,128)S(1)}, f32[192,256]{0,1:T(8,128)S(1)}, u32[]{:S(2)}, u32[]{:S(2)}) %collective-permute-start.14) | collective-permute-done | bytes 196640 | tf_op jit(solution)/shard_map/ppermute | solution.py:17
  (73 shorter events, 34.0 us)
Async XLA Ops:
  0.6 44.9 %copy-start.3 = (s32[1,192]{1,0:T(1,128)S(1)}, s32[1,192]{1,0:T(1,128)}, u32[]{:S(2)}) copy-start(s32[1,192]{1,0:T(1,128)} %param.11) | copy-start | bytes 2308
  0.6 36.1 %copy-start = (bf16[1,192,256]{2,1,0:T(8,128)(2,1)S(1)}, bf16[1,192,256]{2,1,0:T(8,128)(2,1)}, u32[]{:S(2)}) copy-start(bf16[1,192,256]{2,1,0:T(8,128)(2,1)} %param.8) | copy-start | bytes 294916
  0.7 45.2 %copy-start.1 = (bf16[1,192,256]{2,1,0:T(8,128)(2,1)S(1)}, bf16[1,192,256]{2,1,0:T(8,128)(2,1)}, u32[]{:S(2)}) copy-start(bf16[1,192,256]{2,1,0:T(8,128)(2,1)} %param.9) | copy-start | bytes 294916
  0.7 28.3 %collective-permute-start.6 = (s32[192]{0:T(256)}, s32[192]{0:T(256)S(1)}, u32[]{:S(2)}, u32[]{:S(2)}) collective-permute-start(s32[192]{0:T(256)} %bitcast.116), channel_id=1, source_target_pairs={{0,384},{384,0},{1,385},{385,1},{2,386},{386,2},{3,387},{387,3},{4... | collective-permute-start | bytes 2312 | tf_op jit(solution)/shard_map/ppermute | solution.py:17
  7.7 13.6 %collective-permute-start.3 = (s32[192]{0:T(256)S(1)}, s32[192]{0:T(256)S(1)}, u32[]{:S(2)}, u32[]{:S(2)}) collective-permute-start(s32[192]{0:T(256)S(1)} %broadcast_select_fusion.6), channel_id=1, source_target_pairs={{0,384},{384,0},{1,385},{385,1},{2,386},{386,2},{3,387},{387,3},{4... | collective-permute-start | bytes 2312 | tf_op jit(solution)/shard_map/ppermute | solution.py:17
  9.9 26.8 %collective-permute-start.9 = (bf16[192,256]{1,0:T(8,128)(2,1)}, bf16[192,256]{1,0:T(8,128)(2,1)S(1)}, u32[]{:S(2)}, u32[]{:S(2)}) collective-permute-start(bf16[192,256]{1,0:T(8,128)(2,1)} %bitcast.108), channel_id=1, source_target_pairs={{0,384},{384,0},{1,385},{385,1},{2,386},{386,2},{3,387},{387,3},{4... | collective-permute-start | bytes 294920 | tf_op jit(solution)/shard_map/ppermute | solution.py:17
  14.5 31.4 %collective-permute-start = (bf16[192,256]{1,0:T(8,128)(2,1)}, bf16[192,256]{1,0:T(8,128)(2,1)S(1)}, u32[]{:S(2)}, u32[]{:S(2)}) collective-permute-start(bf16[192,256]{1,0:T(8,128)(2,1)} %bitcast.111), channel_id=1, source_target_pairs={{0,384},{384,0},{1,385},{385,1},{2,386},{386,2},{3,387},{387,3},{4... | collective-permute-start | bytes 294920 | tf_op jit(solution)/shard_map/ppermute | solution.py:17
  21.4 10.2 %collective-permute-start.5 = (s32[384]{0:T(512)S(1)}, s32[384]{0:T(512)S(1)}, u32[]{:S(2)}, u32[]{:S(2)}) collective-permute-start(s32[384]{0:T(512)S(1)} %pad_add_fusion), channel_id=1, source_target_pairs={{0,2},{1,3},{2,4},{3,5},{4,6},{5,7},{6,8},{7,9},{8,10},{9,11},{10,... | collective-permute-start | bytes 4616 | tf_op jit(solution)/shard_map/ppermute | solution.py:27
  23.8 11.1 %collective-permute-start.4 = (s32[384]{0:T(512)S(1)}, s32[384]{0:T(512)S(1)}, u32[]{:S(2)}, u32[]{:S(2)}) collective-permute-start(s32[384]{0:T(512)S(1)} %pad_add_fusion), channel_id=1, source_target_pairs={{0,1},{1,2},{2,3},{3,4},{4,5},{5,6},{6,7},{7,8},{8,9},{9,10},{10,1... | collective-permute-start | bytes 4616 | tf_op jit(solution)/shard_map/ppermute | solution.py:27
  29.7 5.3 %collective-permute-start.7 = (s32[384]{0:T(512)S(1)}, s32[384]{0:T(512)S(1)}, u32[]{:S(2)}, u32[]{:S(2)}) collective-permute-start(s32[384]{0:T(512)S(1)} %pad_add_fusion.1), channel_id=1, source_target_pairs={{0,1},{1,2},{2,3},{3,4},{4,5},{5,6},{6,7},{7,8},{8,9},{9,10},{10,1... | collective-permute-start | bytes 4616 | tf_op jit(solution)/shard_map/ppermute | solution.py:27
  31.6 4.3 %collective-permute-start.8 = (s32[384]{0:T(512)S(1)}, s32[384]{0:T(512)S(1)}, u32[]{:S(2)}, u32[]{:S(2)}) collective-permute-start(s32[384]{0:T(512)S(1)} %pad_add_fusion.1), channel_id=1, source_target_pairs={{0,2},{1,3},{2,4},{3,5},{4,6},{5,7},{6,8},{7,9},{8,10},{9,11},{10,... | collective-permute-start | bytes 4616 | tf_op jit(solution)/shard_map/ppermute | solution.py:27
  36.7 15.0 %collective-permute-start.10 = (bf16[384,256]{1,0:T(8,128)(2,1)S(1)}, bf16[384,256]{1,0:T(8,128)(2,1)S(1)}, u32[]{:S(2)}, u32[]{:S(2)}) collective-permute-start(bf16[384,256]{1,0:T(8,128)(2,1)S(1)} %pad_maximum_fusion.7), channel_id=1, source_target_pairs={{0,1},{1,2},{2,3},{3,4},{4,5},{5,6},{6,7},{7,8},{8,9},{9,10},{10,1... | collective-permute-start | bytes 589832 | tf_op jit(solution)/shard_map/ppermute | solution.py:27
  43.6 8.2 %collective-permute-start.11 = (bf16[384,256]{1,0:T(8,128)(2,1)S(1)}, bf16[384,256]{1,0:T(8,128)(2,1)S(1)}, u32[]{:S(2)}, u32[]{:S(2)}) collective-permute-start(bf16[384,256]{1,0:T(8,128)(2,1)S(1)} %pad_maximum_fusion.7), channel_id=1, source_target_pairs={{0,2},{1,3},{2,4},{3,5},{4,6},{5,7},{6,8},{7,9},{8,10},{9,11},{10,... | collective-permute-start | bytes 589832 | tf_op jit(solution)/shard_map/ppermute | solution.py:27
  45.9 11.8 %collective-permute-start.1 = (bf16[384,256]{1,0:T(8,128)(2,1)S(1)}, bf16[384,256]{1,0:T(8,128)(2,1)S(1)}, u32[]{:S(2)}, u32[]{:S(2)}) collective-permute-start(bf16[384,256]{1,0:T(8,128)(2,1)S(1)} %pad_maximum_fusion.6), channel_id=1, source_target_pairs={{0,1},{1,2},{2,3},{3,4},{4,5},{5,6},{6,7},{7,8},{8,9},{9,10},{10,1... | collective-permute-start | bytes 589832 | tf_op jit(solution)/shard_map/ppermute | solution.py:27
  47.9 9.8 %collective-permute-start.2 = (bf16[384,256]{1,0:T(8,128)(2,1)S(1)}, bf16[384,256]{1,0:T(8,128)(2,1)S(1)}, u32[]{:S(2)}, u32[]{:S(2)}) collective-permute-start(bf16[384,256]{1,0:T(8,128)(2,1)S(1)} %pad_maximum_fusion.6), channel_id=1, source_target_pairs={{0,2},{1,3},{2,4},{3,5},{4,6},{5,7},{6,8},{7,9},{8,10},{9,11},{10,... | collective-permute-start | bytes 589832 | tf_op jit(solution)/shard_map/ppermute | solution.py:27
  63.0 2.3 %copy-start.2 = (bf16[192,1,7,128]{3,2,1,0:T(8,128)(2,1)S(1)}, bf16[192,1,7,128]{3,2,1,0:T(8,128)(2,1)}, u32[]{:S(2)}) copy-start(bf16[192,1,7,128]{3,2,1,0:T(8,128)(2,1)} %get-tuple-element.25) | copy-start | bytes 1032196
  67.9 23.3 %collective-permute-start.15 = (f32[384,256]{0,1:T(8,128)}, f32[384,256]{0,1:T(8,128)}, u32[]{:S(2)}, u32[]{:S(2)}) collective-permute-start(f32[384,256]{0,1:T(8,128)} %get-tuple-element.20), channel_id=1, source_target_pairs={{1,0},{2,1},{3,2},{4,3},{5,4},{6,5},{7,6},{8,7},{9,8},{10,9},{11,1... | collective-permute-start | bytes 1179656 | tf_op jit(solution)/shard_map/ppermute | solution.py:27
  70.3 20.9 %collective-permute-start.16 = (f32[384,256]{0,1:T(8,128)}, f32[384,256]{0,1:T(8,128)}, u32[]{:S(2)}, u32[]{:S(2)}) collective-permute-start(f32[384,256]{0,1:T(8,128)} %get-tuple-element.21), channel_id=1, source_target_pairs={{2,0},{3,1},{4,2},{5,3},{6,4},{7,5},{8,6},{9,7},{10,8},{11,9},{12,... | collective-permute-start | bytes 1179656 | tf_op jit(solution)/shard_map/ppermute | solution.py:27
  80.0 17.2 %collective-permute-start.12 = (f32[384,256]{0,1:T(8,128)}, f32[384,256]{0,1:T(8,128)S(1)}, u32[]{:S(2)}, u32[]{:S(2)}) collective-permute-start(f32[384,256]{0,1:T(8,128)} %get-tuple-element.22), channel_id=1, source_target_pairs={{1,0},{2,1},{3,2},{4,3},{5,4},{6,5},{7,6},{8,7},{9,8},{10,9},{11,1... | collective-permute-start | bytes 1179656 | tf_op jit(solution)/shard_map/ppermute | solution.py:27
  82.7 15.5 %collective-permute-start.13 = (f32[384,256]{0,1:T(8,128)}, f32[384,256]{0,1:T(8,128)}, u32[]{:S(2)}, u32[]{:S(2)}) collective-permute-start(f32[384,256]{0,1:T(8,128)} %get-tuple-element.23), channel_id=1, source_target_pairs={{2,0},{3,1},{4,2},{5,3},{6,4},{7,5},{8,6},{9,7},{10,8},{11,9},{12,... | collective-permute-start | bytes 1179656 | tf_op jit(solution)/shard_map/ppermute | solution.py:27
  92.5 22.3 %collective-permute-start.17 = (f32[192,256]{0,1:T(8,128)S(1)}, f32[192,256]{0,1:T(8,128)S(1)}, u32[]{:S(2)}, u32[]{:S(2)}) collective-permute-start(f32[192,256]{0,1:T(8,128)S(1)} %slice.93), channel_id=1, source_target_pairs={{0,384},{384,0},{1,385},{385,1},{2,386},{386,2},{3,387},{387,3},{4... | collective-permute-start | bytes 589832 | tf_op jit(solution)/shard_map/ppermute | solution.py:17
  99.4 21.0 %collective-permute-start.14 = (f32[192,256]{0,1:T(8,128)S(1)}, f32[192,256]{0,1:T(8,128)S(1)}, u32[]{:S(2)}, u32[]{:S(2)}) collective-permute-start(f32[192,256]{0,1:T(8,128)S(1)} %slice.87), channel_id=1, source_target_pairs={{0,384},{384,0},{1,385},{385,1},{2,386},{386,2},{3,387},{387,3},{4... | collective-permute-start | bytes 589832 | tf_op jit(solution)/shard_map/ppermute | solution.py:17
where the time goes:
time: 122 us; the launch traced here: 121 us
  starting transfers between devices  60.6 us (50%)
  matrix products  18.6 us (15%)
  waiting for transfers between devices  18 us (15%)
  local copies, waits for them, and re-layouts  11.3 us (9%)
  other arithmetic  10.9 us (9%)
  between operations  1.78 us (1%)
    ppermute x12, starting transfers between devices, from_behind(): return lax.ppermute(block, axis, route)  37.9 us
    ppermute x6, starting transfers between devices, partner(): return lax.ppermute(block, axis, route)  22.7 us
    ppermute x6, waiting for transfers between devices, partner(): return lax.ppermute(block, axis, route)  15.9 us
    dot_general x2, matrix products, head_backward(): jnp.einsum('qgd,kd->gqk', dh, vh, preferred_element_type=jnp.float32)  4.7 us
    dot_general x2, matrix products, head_forward(): jnp.einsum('gqk,kd->qgd', weights, vh, preferred_element_type=jnp.float32)  4.32 us
    dot_general x2, matrix products, head_backward(): jnp.einsum('gqk,qgd->kd', prob.astype(jnp.bfloat16), dh, preferred_elemen...  3.24 us
    dot_general x2, matrix products, head_forward(): jnp.einsum('qgd,kd->gqk', qh, kh, preferred_element_type=jnp.float32)  2.93 us
    reduce_sum x2, other arithmetic, head_forward(): total = jnp.sum(expo, axis=-1)  2.58 us
  transfers between devices with their start and end apart: 18, of which 4 were waited for; matrix products, arithmetic and copies ran while one was open for 25% of the time, Pallas kernels for 0%

commit v1 on v0

v1 whole, which is shorter than its diff:
```python
import jax
import jax.numpy as jnp
from jax import lax
from jax.experimental import pallas as pl
from jax.experimental.pallas import tpu as pltpu
from jax.sharding import PartitionSpec as P

TOKENS = 192
HEAD = 128
SHARING = 7
KEY_HEADS = 2
BLOCK = 336
PIECES = 6
WINDOW = PIECES * TOKENS
META = 16
ROWS = TOKENS + META
KV = 2 * KEY_HEADS * HEAD
F32 = jnp.float32
BF16 = jnp.bfloat16
SCALE = HEAD**-0.5
LOG2E = 1.4426950408889634
VMEM = pl.BlockSpec(memory_space=pltpu.VMEM)
SMEM = pl.BlockSpec(memory_space=pltpu.SMEM)


def dot(a, b, contract):
    return lax.dot_general(a, b, (contract, ((), ())), preferred_element_type=F32)


def nt(a, b):
    return dot(a, b, ((1,), (1,)))


def nn(a, b):
    return dot(a, b, ((1,), (0,)))


def tn(a, b):
    return dot(a, b, ((0,), (0,)))


def pack_kernel(keys, values, slot_pos, counts, seg_id, packed):
    half = KEY_HEADS * HEAD
    packed[0:TOKENS, 0:half] = keys[0]
    packed[0:TOKENS, half:KV] = values[0]
    pos = slot_pos[...].astype(F32)
    local = pos - jnp.floor((pos + 0.5) * (1.0 / BLOCK)) * BLOCK
    local = local.astype(jnp.int32)
    live = lax.broadcasted_iota(jnp.int32, (1, TOKENS), 1) < counts[0, 0]
    place = lax.broadcasted_iota(jnp.int32, (BLOCK, TOKENS), 0)
    onehot = jnp.where((place == local) & live, 1.0, 0.0).astype(BF16)
    seg = seg_id[...] + 1
    digit = lax.broadcasted_iota(jnp.int32, (META, BLOCK), 0)
    low = (seg & 255).astype(F32)
    high = (seg >> 8).astype(F32)
    digits = jnp.where(digit == 2, low, jnp.where(digit == 3, high, 0.0))
    facts = nn(digits.astype(BF16), onehot)
    row = lax.broadcasted_iota(jnp.int32, (META, TOKENS), 0)
    live_pos = jnp.where(live, local, 0)
    facts = jnp.where(row == 0, (live_pos & 255).astype(F32), facts)
    facts = jnp.where(row == 1, (live_pos >> 8).astype(F32), facts)
    packed[TOKENS:ROWS, :] = jnp.zeros((META, KV), BF16)
    packed[TOKENS:ROWS, 0:TOKENS] = facts.astype(BF16)


def pack(keys, values, slot_pos, counts, seg_id):
    return pl.pallas_call(
        pack_kernel,
        out_shape=jax.ShapeDtypeStruct((ROWS, KV), BF16),
        in_specs=[VMEM, VMEM, VMEM, SMEM, VMEM],
        out_specs=VMEM,
    )(keys, values, slot_pos, counts, seg_id)


def fill_bias(pieces, bias):
    eye = lax.broadcasted_iota(jnp.int32, (TOKENS, TOKENS), 0) == lax.broadcasted_iota(jnp.int32, (TOKENS, TOKENS), 1)
    columns = nt(eye.astype(BF16), pieces[0][TOKENS:ROWS, 0:TOKENS])
    query_pos = columns[:, 0:1] + columns[:, 1:2] * 256.0
    query_seg = columns[:, 2:3] + columns[:, 3:4] * 256.0
    live = query_seg > 0.5
    wanted = jnp.where(live, query_seg, -1.0)
    for at in range(PIECES):
        facts = pieces[at][TOKENS:ROWS, 0:TOKENS].astype(F32)
        visible = facts[2:3] + facts[3:4] * 256.0 == wanted
        if at < 2:
            visible = visible & (facts[0:1] + facts[1:2] * 256.0 <= query_pos)
        bias[:, at * TOKENS : (at + 1) * TOKENS] = jnp.where(visible, 0.0, -1e30)
    return live


def attention_kernel(queries, grads, *refs):
    pieces = refs[:PIECES]
    attended, grad_queries = refs[PIECES : PIECES + 2]
    returned = refs[PIECES + 2 : 2 * PIECES + 2]
    keys, values, bias, grad_keys, grad_values = refs[2 * PIECES + 2 :]
    for at in range(PIECES):
        for h in range(KEY_HEADS):
            span = pl.ds(at * TOKENS, TOKENS)
            keys[h, span, :] = pieces[at][0:TOKENS, h * HEAD : (h + 1) * HEAD]
            values[h, span, :] = pieces[at][0:TOKENS, (KEY_HEADS + h) * HEAD : (KEY_HEADS + h + 1) * HEAD]
    live = fill_bias(pieces, bias)
    for g in range(SHARING):
        for h in range(KEY_HEADS):
            column = pl.ds((h * SHARING + g) * HEAD, HEAD)
            key, value = keys[h], values[h]
            query, grad = queries[0, :, column], grads[0, :, column]
            scores = nt(query, key) * (SCALE * LOG2E) + bias[...]
            top = jnp.max(scores, axis=1, keepdims=True)
            expo = jnp.exp2(scores - top)
            total = jnp.sum(expo, axis=1, keepdims=True)
            prob = expo * jnp.where(live, 1.0 / total, 0.0)
            prob_b = prob.astype(BF16)
            result = nn(prob_b, value).astype(BF16)
            attended[0, :, column] = result
            delta = jnp.sum(result.astype(F32) * grad.astype(F32), axis=1, keepdims=True)
            dscore = (prob * (nt(grad, value) - delta)).astype(BF16)
            grad_queries[0, :, column] = (nn(dscore, key) * SCALE).astype(BF16)
            grad_value = tn(grad, prob_b)
            grad_key = tn(query, dscore)
            if g == 0:
                grad_values[h] = grad_value
                grad_keys[h] = grad_key
            else:
                grad_values[h] += grad_value
                grad_keys[h] += grad_key
    for h in range(KEY_HEADS):
        grad_key = grad_keys[h].T * SCALE
        grad_value = grad_values[h].T
        for at in range(PIECES):
            span = slice(at * TOKENS, (at + 1) * TOKENS)
            returned[at][:, h * HEAD : (h + 1) * HEAD] = grad_key[span].astype(BF16)
            returned[at][:, (KEY_HEADS + h) * HEAD : (KEY_HEADS + h + 1) * HEAD] = grad_value[span].astype(BF16)


def attention(queries, grads, pieces):
    wide = jax.ShapeDtypeStruct(queries.shape, BF16)
    return pl.pallas_call(
        attention_kernel,
        out_shape=[wide, wide] + [jax.ShapeDtypeStruct((TOKENS, KV), BF16)] * PIECES,
        in_specs=[VMEM] * (2 + PIECES),
        out_specs=[VMEM] * (2 + PIECES),
        scratch_shapes=[
            pltpu.VMEM((KEY_HEADS, WINDOW, HEAD), BF16),
            pltpu.VMEM((KEY_HEADS, WINDOW, HEAD), BF16),
            pltpu.VMEM((TOKENS, WINDOW), F32),
            pltpu.VMEM((KEY_HEADS, HEAD, WINDOW), F32),
            pltpu.VMEM((KEY_HEADS, HEAD, WINDOW), F32),
        ],
        compiler_params=pltpu.CompilerParams(vmem_limit_bytes=48 * 2**20),
        cost_estimate=pl.CostEstimate(flops=4_800_000_000, bytes_accessed=6_000_000, transcendentals=3_100_000),
    )(queries, grads, *pieces)


BLOCKS = ("seq", "tp")
ALL = ("grp", "seq", "tp")


def shift_blocks(array, distance):
    count = lax.axis_size(BLOCKS)
    route = [(i, i + distance) for i in range(count) if 0 <= i + distance < count]
    return lax.ppermute(array, BLOCKS, route)


def shift_across(array, distance):
    count = lax.axis_size(BLOCKS)
    route = [
        (g * count + i, (1 - g) * count + i + distance)
        for g in range(2)
        for i in range(count)
        if 0 <= i + distance < count
    ]
    return lax.ppermute(array, ALL, route)


def exchange(array):
    return lax.ppermute(array, "grp", [(0, 1), (1, 0)])


def swap_cores(array):
    count = lax.axis_size(BLOCKS)
    return lax.ppermute(array, BLOCKS, [(i, i ^ 1) for i in range(count)])


def body(queries, keys, values, grad_out, slot_pos, counts, seg_id):
    core = lax.axis_index(BLOCKS) % 2
    own = pack(keys, values, slot_pos, counts, seg_id.reshape(1, BLOCK))
    behind = shift_blocks(own, 2)
    other = exchange(own)
    across = shift_across(own, 2)
    first = jnp.where(core == 0, jnp.stack([own, other]), jnp.stack([behind, across]))
    swapped = swap_cores(first)
    pieces = (own, other, swapped[0], swapped[1], behind, across)
    attended, grad_queries, *parts = attention(queries, grad_out, pieces)
    back = swap_cores(jnp.stack([parts[2], parts[3]])).astype(F32)
    near = jnp.where(core == 0, back, 0.0)
    far = jnp.where(core == 0, 0.0, back)
    from_ahead = shift_blocks((parts[4].astype(F32) + far[0]).astype(BF16), -2)
    from_across = shift_across((parts[5].astype(F32) + far[1]).astype(BF16), -2)
    from_other = exchange((parts[1].astype(F32) + near[1]).astype(BF16))
    total = parts[0].astype(F32) + near[0] + from_ahead.astype(F32) + from_across.astype(F32) + from_other.astype(F32)
    total = total.astype(BF16)
    half = KEY_HEADS * HEAD
    return attended, grad_queries, total[None, :, :half], total[None, :, half:]


def solution(mesh):
    rows = P("grp", BLOCKS, None)
    slots = P("grp", BLOCKS)
    return jax.shard_map(
        body,
        mesh=mesh,
        in_specs=(rows, rows, rows, rows, slots, slots, P(BLOCKS)),
        out_specs=(rows, rows, rows, rows),
        check_vma=False,
    )
```

time: 122 us -> 75 us (0.61)
  the two profiles are of different devices: /device:TPU:249 before, /device:TPU:250 now
where the time goes in v1:
time: 75 us; the launch traced here: 74.6 us
  waiting for transfers between devices  24.6 us (33%)
  starting transfers between devices  24.3 us (32%)
  Pallas kernels  20.6 us (27%)
  local copies, waits for them, and re-layouts  1.98 us (3%)
  other arithmetic  1.64 us (2%)
  between operations  1.45 us (2%)
    pallas_call x1, Pallas kernels, attention(): pl.pallas_call(attention_kernel, out_shape=[wide, wide] + [jax.ShapeDtype...  18.8 us
    ppermute x2, waiting for transfers between devices, exchange(): return lax.ppermute(array, 'grp', [(0, 1), (1, 0)])  12.1 us
    ppermute x2, starting transfers between devices, shift_across(): return lax.ppermute(array, ALL, route)  9.22 us
    ppermute x2, starting transfers between devices, shift_blocks(): return lax.ppermute(array, BLOCKS, route)  6.91 us
    ppermute x2, waiting for transfers between devices, shift_across(): return lax.ppermute(array, ALL, route)  5.99 us
    ppermute x2, starting transfers between devices, exchange(): return lax.ppermute(array, 'grp', [(0, 1), (1, 0)])  4.12 us
    ppermute x2, starting transfers between devices, swap_cores(): return lax.ppermute(array, BLOCKS, [(i, i ^ 1) for i in range(count)])  4.09 us
    ppermute x2, waiting for transfers between devices, swap_cores(): return lax.ppermute(array, BLOCKS, [(i, i ^ 1) for i in range(count)])  3.3 us
  transfers between devices with their start and end apart: 8, of which 7 were waited for; matrix products, arithmetic and copies ran while one was open for 0% of the time, Pallas kernels for 0%

profile of v1, /device:TPU:250, one launch (start us, length us, event | category | flops | bytes accessed | tf_op | source)
XLA Modules:
  0.0 74.6 jit_solution(6765710990701769310)
XLA Ops:
  1.3 1.2 %reshape.11.seg_id = s32[1,336]{1,0:T(1,128)} reshape(s32[336]{0:T(512)} %param.13) | data formatting | bytes 2688 | tf_op jit(solution)/shard_map/reshape | solution.py:186
  2.5 1.8 %shard_map.102.refs_0_ = bf16[208,512]{1,0:T(8,128)(2,1)} custom-call(bf16[1,192,256]{2,1,0:T(8,128)(2,1)} %keys.1, bf16[1,192,256]{2,1,0:T(8,128)(2,1)} %values.1, s32[1,192]{1,0:T(1,128)} %slot_pos.1, s32[1,1]{1,0:T(1,128)S(6)} %copy.11.counts, s32[1,336]{1,0:T(1,128)} %reshape.11.seg_id), custom_call_target="tpu_custom_call" | custom-call | tf_op jit(solution)/shard_map/pallas_call | solution.py:67
  4.3 5.6 %collective-permute-start.2 = (bf16[208,512]{1,0:T(8,128)(2,1)}, bf16[208,512]{1,0:T(8,128)(2,1)S(1)}, u32[]{:S(2)}, u32[]{:S(2)}) collective-permute-start(bf16[208,512]{1,0:T(8,128)(2,1)} %shard_map.102.refs_0_), channel_id=1, source_target_pairs={{0,386},{1,387},{2,388},{3,389},{4,390},{5,391},{6,392},{7,393},{8... | collective-permute-start | bytes 638984 | tf_op jit(solution)/shard_map/ppermute | solution.py:172
  9.9 5.0 %collective-permute-start.1 = (bf16[208,512]{1,0:T(8,128)(2,1)}, bf16[208,512]{1,0:T(8,128)(2,1)S(1)}, u32[]{:S(2)}, u32[]{:S(2)}) collective-permute-start(bf16[208,512]{1,0:T(8,128)(2,1)} %shard_map.102.refs_0_), channel_id=1, source_target_pairs={{0,2},{1,3},{2,4},{3,5},{4,6},{5,7},{6,8},{7,9},{8,10},{9,11},{10,... | collective-permute-start | bytes 638984 | tf_op jit(solution)/shard_map/ppermute | solution.py:161
  14.9 1.9 %collective-permute-start = (bf16[208,512]{1,0:T(8,128)(2,1)}, bf16[208,512]{1,0:T(8,128)(2,1)S(1)}, u32[]{:S(2)}, u32[]{:S(2)}) collective-permute-start(bf16[208,512]{1,0:T(8,128)(2,1)} %shard_map.102.refs_0_), channel_id=1, source_target_pairs={{0,384},{384,0},{1,385},{385,1},{2,386},{386,2},{3,387},{387,3},{4... | collective-permute-start | bytes 638984 | tf_op jit(solution)/shard_map/ppermute | solution.py:176
  16.9 2.6 %collective-permute-done.1.refs_4_ = bf16[208,512]{1,0:T(8,128)(2,1)S(1)} collective-permute-done((bf16[208,512]{1,0:T(8,128)(2,1)}, bf16[208,512]{1,0:T(8,128)(2,1)S(1)}, u32[]{:S(2)}, u32[]{:S(2)}) %collective-permute-start.1) | collective-permute-done | bytes 213024 | tf_op jit(solution)/shard_map/ppermute | solution.py:161
  19.5 5.4 %collective-permute-done.refs_1_ = bf16[208,512]{1,0:T(8,128)(2,1)S(1)} collective-permute-done((bf16[208,512]{1,0:T(8,128)(2,1)}, bf16[208,512]{1,0:T(8,128)(2,1)S(1)}, u32[]{:S(2)}, u32[]{:S(2)}) %collective-permute-start) | collective-permute-done | bytes 213024 | tf_op jit(solution)/shard_map/ppermute | solution.py:176
  25.0 1.1 %maximum_select_fusion = bf16[2,208,512]{2,1,0:T(8,128)(2,1)S(1)} fusion(bf16[1,208,512]{2,1,0:T(8,128)(2,1)S(1)} %bitcast.47, bf16[1,208,512]{2,1,0:T(8,128)(2,1)} %bitcast.44, bf16[1,208,512]{2,1,0:T(8,128)(2,1)S(1)} %bitcast.45, bf16[1,208,512]{2,1,0:T(8,128)(2,1)S(1)} %bitcast.46, pred[]{:T(512)S(6)} %eq.4), kind=kLoop, calls=%fused_computation.2 | loop fusion | flops 638976 | bytes 1277953 | tf_op jit(solution)/shard_map/jit(_where)/select_n | solution.py:190
  26.1 0.0 copy-start
  26.1 2.1 %collective-permute-start.3 = (bf16[2,208,512]{2,1,0:T(8,128)(2,1)S(1)}, bf16[2,208,512]{2,1,0:T(8,128)(2,1)S(1)}, u32[]{:S(2)}, u32[]{:S(2)}) collective-permute-start(bf16[2,208,512]{2,1,0:T(8,128)(2,1)S(1)} %maximum_select_fusion), channel_id=1, source_target_pairs={{0,1},{1,0},{2,3},{3,2},{4,5},{5,4},{6,7},{7,6},{8,9},{9,8},{10,11... | collective-permute-start | bytes 1277960 | tf_op jit(solution)/shard_map/ppermute | solution.py:181
  28.2 1.7 %collective-permute-done.3 = bf16[2,208,512]{2,1,0:T(8,128)(2,1)S(1)} collective-permute-done((bf16[2,208,512]{2,1,0:T(8,128)(2,1)S(1)}, bf16[2,208,512]{2,1,0:T(8,128)(2,1)S(1)}, u32[]{:S(2)}, u32[]{:S(2)}) %collective-permute-start.3) | collective-permute-done | bytes 426016 | tf_op jit(solution)/shard_map/ppermute | solution.py:181
  30.0 18.8 %shard_map.103 = (bf16[1,192,1792]{2,1,0:T(8,128)(2,1)}, bf16[1,192,1792]{2,1,0:T(8,128)(2,1)}, bf16[192,512]{1,0:T(8,128)(2,1)S(1)}, bf16[192,512]{1,0:T(8,128)...) custom-call(bf16[1,192,1792]{2,1,0:T(8,128)(2,1)S(1)} %copy-done.1, ...), custom_call_target="tpu_custom_call" | custom-call | flops 4800000000 | bytes 6000000 | tf_op jit(solution)/shard_map/pallas_call | solution.py:137
  48.8 2.0 %collective-permute-start.4 = (bf16[2,192,512]{2,1,0:T(8,128)(2,1)S(1)}, bf16[2,192,512]{2,1,0:T(8,128)(2,1)S(1)}, u32[]{:S(2)}, u32[]{:S(2)}) collective-permute-start(bf16[2,192,512]{2,1,0:T(8,128)(2,1)S(1)} %pad_maximum_fusion), channel_id=1, source_target_pairs={{0,1},{1,0},{2,3},{3,2},{4,5},{5,4},{6,7},{7,6},{8,9},{9,8},{10,11... | collective-permute-start | bytes 1179656 | tf_op jit(solution)/shard_map/ppermute | solution.py:181
  50.8 1.6 %collective-permute-done.4 = bf16[2,192,512]{2,1,0:T(8,128)(2,1)S(1)} collective-permute-done((bf16[2,192,512]{2,1,0:T(8,128)(2,1)S(1)}, bf16[2,192,512]{2,1,0:T(8,128)(2,1)S(1)}, u32[]{:S(2)}, u32[]{:S(2)}) %collective-permute-start.4) | collective-permute-done | bytes 393248 | tf_op jit(solution)/shard_map/ppermute | solution.py:181
  52.4 0.2 convert_select_fusion
  52.7 2.2 %collective-permute-start.7 = (bf16[192,512]{1,0:T(8,128)(2,1)S(1)}, bf16[192,512]{1,0:T(8,128)(2,1)S(1)}, u32[]{:S(2)}, u32[]{:S(2)}) collective-permute-start(bf16[192,512]{1,0:T(8,128)(2,1)S(1)} %fusion.1), channel_id=1, source_target_pairs={{0,384},{384,0},{1,385},{385,1},{2,386},{386,2},{3,387},{387,3},{4... | collective-permute-start | bytes 589832 | tf_op jit(solution)/shard_map/ppermute | solution.py:176
  54.9 0.1 fusion.5
  55.0 1.9 %collective-permute-start.5 = (bf16[192,512]{1,0:T(8,128)(2,1)S(1)}, bf16[192,512]{1,0:T(8,128)(2,1)S(1)}, u32[]{:S(2)}, u32[]{:S(2)}) collective-permute-start(bf16[192,512]{1,0:T(8,128)(2,1)S(1)} %get-tuple-element.20), channel_id=1, source_target_pairs={{2,0},{3,1},{4,2},{5,3},{6,4},{7,5},{8,6},{9,7},{10,8},{11,9},{12,... | collective-permute-start | bytes 589832 | tf_op jit(solution)/shard_map/ppermute | solution.py:161
  56.9 3.6 %collective-permute-start.6 = (bf16[192,512]{1,0:T(8,128)(2,1)S(1)}, bf16[192,512]{1,0:T(8,128)(2,1)S(1)}, u32[]{:S(2)}, u32[]{:S(2)}) collective-permute-start(bf16[192,512]{1,0:T(8,128)(2,1)S(1)} %get-tuple-element.21), channel_id=1, source_target_pairs={{2,384},{3,385},{4,386},{5,387},{6,388},{7,389},{8,390},{9,391},{1... | collective-permute-start | bytes 589832 | tf_op jit(solution)/shard_map/ppermute | solution.py:172
  60.5 6.7 %collective-permute-done.7 = bf16[192,512]{1,0:T(8,128)(2,1)S(1)} collective-permute-done((bf16[192,512]{1,0:T(8,128)(2,1)S(1)}, bf16[192,512]{1,0:T(8,128)(2,1)S(1)}, u32[]{:S(2)}, u32[]{:S(2)}) %collective-permute-start.7) | collective-permute-done | bytes 196640 | tf_op jit(solution)/shard_map/ppermute | solution.py:176
  67.2 0.6 collective-permute-done.5
  67.8 6.0 %collective-permute-done.6 = bf16[192,512]{1,0:T(8,128)(2,1)S(1)} collective-permute-done((bf16[192,512]{1,0:T(8,128)(2,1)S(1)}, bf16[192,512]{1,0:T(8,128)(2,1)S(1)}, u32[]{:S(2)}, u32[]{:S(2)}) %collective-permute-start.6) | collective-permute-done | bytes 196640 | tf_op jit(solution)/shard_map/ppermute | solution.py:172
  73.8 0.1 fusion.10
  73.9 0.7 slice_bitcast_fusion.6
  (9 shorter events, 0.1 us)
Async XLA Ops:
  4.3 12.6 %collective-permute-start.2 = (bf16[208,512]{1,0:T(8,128)(2,1)}, bf16[208,512]{1,0:T(8,128)(2,1)S(1)}, u32[]{:S(2)}, u32[]{:S(2)}) collective-permute-start(bf16[208,512]{1,0:T(8,128)(2,1)} %shard_map.102.refs_0_), channel_id=1, source_target_pairs={{0,386},{1,387},{2,388},{3,389},{4,390},{5,391},{6,392},{7,393},{8... | collective-permute-start | bytes 638984 | tf_op jit(solution)/shard_map/ppermute | solution.py:172
  9.9 9.6 %collective-permute-start.1 = (bf16[208,512]{1,0:T(8,128)(2,1)}, bf16[208,512]{1,0:T(8,128)(2,1)S(1)}, u32[]{:S(2)}, u32[]{:S(2)}) collective-permute-start(bf16[208,512]{1,0:T(8,128)(2,1)} %shard_map.102.refs_0_), channel_id=1, source_target_pairs={{0,2},{1,3},{2,4},{3,5},{4,6},{5,7},{6,8},{7,9},{8,10},{9,11},{10,... | collective-permute-start | bytes 638984 | tf_op jit(solution)/shard_map/ppermute | solution.py:161
  14.9 10.0 %collective-permute-start = (bf16[208,512]{1,0:T(8,128)(2,1)}, bf16[208,512]{1,0:T(8,128)(2,1)S(1)}, u32[]{:S(2)}, u32[]{:S(2)}) collective-permute-start(bf16[208,512]{1,0:T(8,128)(2,1)} %shard_map.102.refs_0_), channel_id=1, source_target_pairs={{0,384},{384,0},{1,385},{385,1},{2,386},{386,2},{3,387},{387,3},{4... | collective-permute-start | bytes 638984 | tf_op jit(solution)/shard_map/ppermute | solution.py:176
  25.0 5.0 %copy-start.1 = (bf16[1,192,1792]{2,1,0:T(8,128)(2,1)S(1)}, bf16[1,192,1792]{2,1,0:T(8,128)(2,1)}, u32[]{:S(2)}) copy-start(bf16[1,192,1792]{2,1,0:T(8,128)(2,1)} %queries.1) | copy-start | bytes 2064388
  25.0 5.0 %copy-start.2 = (bf16[1,192,1792]{2,1,0:T(8,128)(2,1)S(1)}, bf16[1,192,1792]{2,1,0:T(8,128)(2,1)}, u32[]{:S(2)}) copy-start(bf16[1,192,1792]{2,1,0:T(8,128)(2,1)} %grads.1) | copy-start | bytes 2064388
  26.1 3.9 %copy-start = (bf16[208,512]{1,0:T(8,128)(2,1)S(1)}, bf16[208,512]{1,0:T(8,128)(2,1)}, u32[]{:S(2)}) copy-start(bf16[208,512]{1,0:T(8,128)(2,1)} %shard_map.102.refs_0_) | copy-start | bytes 638980
  26.1 3.8 %collective-permute-start.3 = (bf16[2,208,512]{2,1,0:T(8,128)(2,1)S(1)}, bf16[2,208,512]{2,1,0:T(8,128)(2,1)S(1)}, u32[]{:S(2)}, u32[]{:S(2)}) collective-permute-start(bf16[2,208,512]{2,1,0:T(8,128)(2,1)S(1)} %maximum_select_fusion), channel_id=1, source_target_pairs={{0,1},{1,0},{2,3},{3,2},{4,5},{5,4},{6,7},{7,6},{8,9},{9,8},{10,11... | collective-permute-start | bytes 1277960 | tf_op jit(solution)/shard_map/ppermute | solution.py:181
  48.8 3.6 %collective-permute-start.4 = (bf16[2,192,512]{2,1,0:T(8,128)(2,1)S(1)}, bf16[2,192,512]{2,1,0:T(8,128)(2,1)S(1)}, u32[]{:S(2)}, u32[]{:S(2)}) collective-permute-start(bf16[2,192,512]{2,1,0:T(8,128)(2,1)S(1)} %pad_maximum_fusion), channel_id=1, source_target_pairs={{0,1},{1,0},{2,3},{3,2},{4,5},{5,4},{6,7},{7,6},{8,9},{9,8},{10,11... | collective-permute-start | bytes 1179656 | tf_op jit(solution)/shard_map/ppermute | solution.py:181
  52.7 14.6 %collective-permute-start.7 = (bf16[192,512]{1,0:T(8,128)(2,1)S(1)}, bf16[192,512]{1,0:T(8,128)(2,1)S(1)}, u32[]{:S(2)}, u32[]{:S(2)}) collective-permute-start(bf16[192,512]{1,0:T(8,128)(2,1)S(1)} %fusion.1), channel_id=1, source_target_pairs={{0,384},{384,0},{1,385},{385,1},{2,386},{386,2},{3,387},{387,3},{4... | collective-permute-start | bytes 589832 | tf_op jit(solution)/shard_map/ppermute | solution.py:176
  55.0 12.8 %collective-permute-start.5 = (bf16[192,512]{1,0:T(8,128)(2,1)S(1)}, bf16[192,512]{1,0:T(8,128)(2,1)S(1)}, u32[]{:S(2)}, u32[]{:S(2)}) collective-permute-start(bf16[192,512]{1,0:T(8,128)(2,1)S(1)} %get-tuple-element.20), channel_id=1, source_target_pairs={{2,0},{3,1},{4,2},{5,3},{6,4},{7,5},{8,6},{9,7},{10,8},{11,9},{12,... | collective-permute-start | bytes 589832 | tf_op jit(solution)/shard_map/ppermute | solution.py:161
  56.9 16.8 %collective-permute-start.6 = (bf16[192,512]{1,0:T(8,128)(2,1)S(1)}, bf16[192,512]{1,0:T(8,128)(2,1)S(1)}, u32[]{:S(2)}, u32[]{:S(2)}) collective-permute-start(bf16[192,512]{1,0:T(8,128)(2,1)S(1)} %get-tuple-element.21), channel_id=1, source_target_pairs={{2,384},{3,385},{4,386},{5,387},{6,388},{7,389},{8,390},{9,391},{1... | collective-permute-start | bytes 589832 | tf_op jit(solution)/shard_map/ppermute | solution.py:172

commit v2 on v1

v2 whole, which is shorter than its diff:
```python
import jax
import jax.numpy as jnp
from jax import lax
from jax.experimental import pallas as pl
from jax.experimental.pallas import tpu as pltpu
from jax.sharding import PartitionSpec as P

TOKENS = 192
HEAD = 128
SHARING = 7
KEY_HEADS = 2
BLOCK = 336
PIECES = 6
WINDOW = PIECES * TOKENS
NEAR = 2 * TOKENS
META = 16
ROWS = TOKENS + META
KV = 2 * KEY_HEADS * HEAD
F32 = jnp.float32
BF16 = jnp.bfloat16
SCALE = HEAD**-0.5
LOG2E = 1.4426950408889634
VMEM = pl.BlockSpec(memory_space=pltpu.VMEM)


def dot(a, b, contract):
    return lax.dot_general(a, b, (contract, ((), ())), preferred_element_type=F32)


def nt(a, b):
    return dot(a, b, ((1,), (1,)))


def nn(a, b):
    return dot(a, b, ((1,), (0,)))


def pack_kernel(keys, values, slot_pos, counts, seg_id, packed):
    half = KEY_HEADS * HEAD
    packed[0:TOKENS, 0:half] = keys[0]
    packed[0:TOKENS, half:KV] = values[0]
    pos = slot_pos[...].astype(F32)
    local = pos - jnp.floor((pos + 0.5) * (1.0 / BLOCK)) * BLOCK
    local = local.astype(jnp.int32)
    live = lax.broadcasted_iota(jnp.int32, (1, TOKENS), 1) < counts[...]
    place = lax.broadcasted_iota(jnp.int32, (BLOCK, TOKENS), 0)
    onehot = jnp.where((place == local) & live, 1.0, 0.0).astype(BF16)
    seg = seg_id[...].reshape(1, BLOCK) + 1
    digit = lax.broadcasted_iota(jnp.int32, (META, BLOCK), 0)
    low = (seg & 255).astype(F32)
    high = (seg >> 8).astype(F32)
    digits = jnp.where(digit == 2, low, jnp.where(digit == 3, high, 0.0))
    facts = nn(digits.astype(BF16), onehot)
    row = lax.broadcasted_iota(jnp.int32, (META, TOKENS), 0)
    live_pos = jnp.where(live, local, 0)
    facts = jnp.where(row == 0, (live_pos & 255).astype(F32), facts)
    facts = jnp.where(row == 1, (live_pos >> 8).astype(F32), facts)
    packed[TOKENS:ROWS, :] = jnp.zeros((META, KV), BF16)
    packed[TOKENS:ROWS, 0:TOKENS] = facts.astype(BF16)


def pack(keys, values, slot_pos, counts, seg_id):
    return pl.pallas_call(
        pack_kernel,
        out_shape=jax.ShapeDtypeStruct((ROWS, KV), BF16),
        in_specs=[VMEM] * 5,
        out_specs=VMEM,
    )(keys, values, slot_pos, counts, seg_id)


def fill_bias(pieces, bias):
    eye = lax.broadcasted_iota(jnp.int32, (TOKENS, TOKENS), 0) == lax.broadcasted_iota(jnp.int32, (TOKENS, TOKENS), 1)
    columns = nt(eye.astype(BF16), pieces[0][TOKENS:ROWS, 0:TOKENS])
    query_pos = columns[:, 0:1] + columns[:, 1:2] * 256.0
    query_seg = columns[:, 2:3] + columns[:, 3:4] * 256.0
    live = query_seg > 0.5
    wanted = jnp.where(live, query_seg, -1.0)
    for at in range(PIECES):
        facts = pieces[at][TOKENS:ROWS, 0:TOKENS].astype(F32)
        visible = facts[2:3] + facts[3:4] * 256.0 == wanted
        if at < 2:
            visible = visible & (facts[0:1] + facts[1:2] * 256.0 <= query_pos)
        bias[:, at * TOKENS : (at + 1) * TOKENS] = jnp.where(visible, 0.0, -1e30)
    return live


def column(n):
    return pl.ds(n * HEAD, HEAD)


def staged(stages, offsets):
    order = [(g, h) for g in range(SHARING) for h in range(KEY_HEADS)]
    for step in range(len(order) + max(offsets)):
        for stage, offset in zip(stages, offsets):
            if 0 <= step - offset < len(order):
                stage(*order[step - offset])


def accumulate(total, h, first, term):
    if first:
        total[h] = term
    else:
        total[h] += term


def turn_kernel(queries, grads, packed, after, queries_here, grads_here, queries_t, grads_t, own):
    queries_here[...] = queries[0]
    grads_here[...] = grads[0]
    own[...] = packed[...]
    for n in range(SHARING * KEY_HEADS):
        queries_t[n] = queries[0, :, column(n)].T
        grads_t[n] = grads[0, :, column(n)].T


def turn(queries, grads, packed, after):
    heads = SHARING * KEY_HEADS
    wide = jax.ShapeDtypeStruct((TOKENS, heads * HEAD), BF16)
    turned = jax.ShapeDtypeStruct((heads, HEAD, TOKENS), BF16)
    return pl.pallas_call(
        turn_kernel,
        out_shape=[wide, wide, turned, turned, jax.ShapeDtypeStruct(packed.shape, BF16)],
        in_specs=[VMEM, VMEM, VMEM, pl.BlockSpec(memory_space=pl.ANY)],
        out_specs=[VMEM] * 5,
        compiler_params=pltpu.CompilerParams(vmem_limit_bytes=16 * 2**20),
        cost_estimate=pl.CostEstimate(flops=0, bytes_accessed=8_000_000, transcendentals=0),
    )(queries, grads, packed, after)


def attention_kernel(queries, grads, queries_t, grads_t, *refs):
    pieces = refs[:PIECES]
    attended, dscores, near_probs, middle, far, keys = refs[PIECES : PIECES + 6]
    values, bias, grad_keys, grad_values = refs[PIECES + 6 :]
    for at in range(PIECES):
        for h in range(KEY_HEADS):
            span = pl.ds(at * TOKENS, TOKENS)
            keys[h, span, :] = pieces[at][0:TOKENS, h * HEAD : (h + 1) * HEAD]
            values[h, span, :] = pieces[at][0:TOKENS, (KEY_HEADS + h) * HEAD : (KEY_HEADS + h + 1) * HEAD]
    live = fill_bias(pieces, bias)
    held = {}

    def products(g, h):
        at = column(h * SHARING + g)
        held[g, h] = nt(queries[:, at], keys[h]), nt(grads[:, at], values[h])

    def softmax(g, h):
        n = h * SHARING + g
        scores, dprob = held[g, h]
        grad = grads[:, column(n)]
        scores = scores * (SCALE * LOG2E) + bias[...]
        top = jnp.max(scores, axis=1, keepdims=True)
        expo = jnp.exp2(scores - top)
        total = jnp.sum(expo, axis=1, keepdims=True)
        prob = expo * jnp.where(live, 1.0 / total, 0.0)
        prob_b = prob.astype(BF16)
        result = nn(prob_b, values[h]).astype(BF16)
        attended[0, :, column(n)] = result
        delta = jnp.sum(result.astype(F32) * grad.astype(F32), axis=1, keepdims=True)
        dscore = (prob * (dprob - delta)).astype(BF16)
        dscores[n] = dscore
        near_probs[n] = prob_b[:, :NEAR]
        held[g, h] = prob_b[:, NEAR:], dscore[:, NEAR:]

    def sums(g, h):
        prob_b, dscore = held.pop((g, h))
        n = h * SHARING + g
        accumulate(grad_values, h, g == 0, nn(grads_t[n], prob_b))
        accumulate(grad_keys, h, g == 0, nn(queries_t[n], dscore))

    staged((products, softmax, sums), (0, 2, 3))
    for h in range(KEY_HEADS):
        grad_key = grad_keys[h].T * SCALE
        grad_value = grad_values[h].T
        for at in range(2):
            span = slice(at * TOKENS, (at + 1) * TOKENS)
            middle[at, :, column(h)] = grad_key[span].astype(BF16)
            middle[at, :, column(KEY_HEADS + h)] = grad_value[span].astype(BF16)
            span = slice((at + 2) * TOKENS, (at + 3) * TOKENS)
            far[at, :, column(h)] = grad_key[span]
            far[at, :, column(KEY_HEADS + h)] = grad_value[span]


def attention(queries, grads, queries_t, grads_t, pieces):
    heads = SHARING * KEY_HEADS
    return pl.pallas_call(
        attention_kernel,
        out_shape=[
            jax.ShapeDtypeStruct((1, TOKENS, heads * HEAD), BF16),
            jax.ShapeDtypeStruct((heads, TOKENS, WINDOW), BF16),
            jax.ShapeDtypeStruct((heads, TOKENS, NEAR), BF16),
            jax.ShapeDtypeStruct((2, TOKENS, KV), BF16),
            jax.ShapeDtypeStruct((2, TOKENS, KV), F32),
            jax.ShapeDtypeStruct((KEY_HEADS, WINDOW, HEAD), BF16),
        ],
        in_specs=[VMEM] * (4 + PIECES),
        out_specs=[VMEM] * 6,
        scratch_shapes=[
            pltpu.VMEM((KEY_HEADS, WINDOW, HEAD), BF16),
            pltpu.VMEM((TOKENS, WINDOW), F32),
            pltpu.VMEM((KEY_HEADS, HEAD, WINDOW - NEAR), F32),
            pltpu.VMEM((KEY_HEADS, HEAD, WINDOW - NEAR), F32),
        ],
        compiler_params=pltpu.CompilerParams(vmem_limit_bytes=32 * 2**20),
        cost_estimate=pl.CostEstimate(flops=3_500_000_000, bytes_accessed=12_000_000, transcendentals=3_100_000),
    )(queries, grads, queries_t, grads_t, *pieces)


def near_kernel(queries_t, grads_t, dscores, probs, near, grad_keys, grad_values):
    def sums(g, h):
        n = h * SHARING + g
        accumulate(grad_values, h, g == 0, nn(grads_t[n], probs[n]))
        accumulate(grad_keys, h, g == 0, nn(queries_t[n], dscores[n, :, :NEAR]))

    staged((sums,), (0,))
    for h in range(KEY_HEADS):
        grad_key = grad_keys[h].T * SCALE
        grad_value = grad_values[h].T
        for at in range(2):
            span = slice(at * TOKENS, (at + 1) * TOKENS)
            near[at, :, column(h)] = grad_key[span]
            near[at, :, column(KEY_HEADS + h)] = grad_value[span]


def near_gradients(queries_t, grads_t, dscores, probs):
    return pl.pallas_call(
        near_kernel,
        out_shape=jax.ShapeDtypeStruct((2, TOKENS, KV), F32),
        in_specs=[VMEM] * 4,
        out_specs=VMEM,
        scratch_shapes=[
            pltpu.VMEM((KEY_HEADS, HEAD, NEAR), F32),
            pltpu.VMEM((KEY_HEADS, HEAD, NEAR), F32),
        ],
        compiler_params=pltpu.CompilerParams(vmem_limit_bytes=24 * 2**20),
        cost_estimate=pl.CostEstimate(flops=530_000_000, bytes_accessed=6_000_000, transcendentals=0),
    )(queries_t, grads_t, dscores, probs)


def query_kernel(dscores, keys, grad_queries):
    for n in range(SHARING * KEY_HEADS):
        grad_queries[0, :, column(n)] = (nn(dscores[n], keys[n // SHARING]) * SCALE).astype(BF16)


def query_gradients(dscores, keys):
    return pl.pallas_call(
        query_kernel,
        out_shape=jax.ShapeDtypeStruct((1, TOKENS, SHARING * KEY_HEADS * HEAD), BF16),
        in_specs=[VMEM] * 2,
        out_specs=VMEM,
        compiler_params=pltpu.CompilerParams(vmem_limit_bytes=24 * 2**20),
        cost_estimate=pl.CostEstimate(flops=800_000_000, bytes_accessed=8_000_000, transcendentals=0),
    )(dscores, keys)


BLOCKS = ("seq", "tp")
ALL = ("grp", "seq", "tp")


def shift_blocks(array, distance):
    count = lax.axis_size(BLOCKS)
    route = [(i, i + distance) for i in range(count) if 0 <= i + distance < count]
    return lax.ppermute(array, BLOCKS, route)


def shift_across(array, distance):
    count = lax.axis_size(BLOCKS)
    route = [
        (g * count + i, (1 - g) * count + i + distance)
        for g in range(2)
        for i in range(count)
        if 0 <= i + distance < count
    ]
    return lax.ppermute(array, ALL, route)


def exchange(array):
    return lax.ppermute(array, "grp", [(0, 1), (1, 0)])


def swap_cores(array):
    count = lax.axis_size(BLOCKS)
    return lax.ppermute(array, BLOCKS, [(i, i ^ 1) for i in range(count)])


def body(queries, keys, values, grad_out, slot_pos, counts, seg_id):
    core = lax.axis_index(BLOCKS) % 2
    packed = pack(keys, values, slot_pos, counts, seg_id)
    other = exchange(packed)
    behind = shift_blocks(packed, 2)
    across = shift_blocks(other, 2)
    *turned, own = turn(queries, grad_out, packed, behind)
    early = swap_cores(jnp.where(core == 0, own, behind))
    late = swap_cores(jnp.where(core == 0, other, across))
    pieces = (own, other, early, late, behind, across)
    attended, dscores, near_probs, middle, far, keys = attention(*turned, pieces)
    back = swap_cores(middle)
    near = near_gradients(turned[2], turned[3], dscores, near_probs)
    back = back.astype(F32)
    far = (far + jnp.where(core == 0, 0.0, back)).astype(BF16)
    near = near + jnp.where(core == 0, back, 0.0)
    far, dscores = lax.optimization_barrier((far, dscores))
    from_across = shift_across(far[1], -2)
    from_other = exchange(near[1].astype(BF16))
    from_ahead = shift_blocks(far[0], -2)
    grad_queries = query_gradients(dscores, keys)
    half = KEY_HEADS * HEAD
    totals = [
        (near[0][:, at] + from_across[:, at].astype(F32) + from_other[:, at].astype(F32) + from_ahead[:, at].astype(F32))
        .astype(BF16)[None]
        for at in (slice(0, half), slice(half, KV))
    ]
    return attended, grad_queries, totals[0], totals[1]


def solution(mesh):
    rows = P("grp", BLOCKS, None)
    slots = P("grp", BLOCKS)
    return jax.shard_map(
        body,
        mesh=mesh,
        in_specs=(rows, rows, rows, rows, slots, slots, P(BLOCKS)),
        out_specs=(rows, rows, rows, rows),
        check_vma=False,
    )
```

time: 75 us -> 70 us (0.933)
  the two profiles are of different devices: /device:TPU:250 before, /device:TPU:1 now
where the time goes in v2:
time: 70 us; the launch traced here: 69.5 us
  starting transfers between devices  38.1 us (54%)
  Pallas kernels  16.1 us (23%)
  waiting for transfers between devices  9.58 us (14%)
  local copies, waits for them, and re-layouts  3.2 us (5%)
  between operations  1.47 us (2%)
  other arithmetic  1.04 us (1%)
    ppermute x3, starting transfers between devices, swap_cores(): return lax.ppermute(array, BLOCKS, [(i, i ^ 1) for i in range(count)])  18.4 us
    pallas_call x1, Pallas kernels, attention(): pl.pallas_call(attention_kernel, out_shape=[jax.ShapeDtypeStruct((1, TOKE...  9.84 us
    ppermute x3, starting transfers between devices, shift_blocks(): return lax.ppermute(array, BLOCKS, route)  9.35 us
    ppermute x2, starting transfers between devices, exchange(): return lax.ppermute(array, 'grp', [(0, 1), (1, 0)])  9.11 us
    ppermute x1, waiting for transfers between devices, shift_across(): return lax.ppermute(array, ALL, route)  4.26 us
    unnamed x6, local copies, waits for them, and re-layouts  3.12 us
    ppermute x3, waiting for transfers between devices, shift_blocks(): return lax.ppermute(array, BLOCKS, route)  2.84 us
    pallas_call x1, Pallas kernels, query_gradients(): pl.pallas_call(query_kernel, out_shape=jax.ShapeDtypeStruct((1, TOKENS, S...  2.61 us
  transfers between devices with their start and end apart: 9, of which 6 were waited for; matrix products, arithmetic and copies ran while one was open for 0% of the time, Pallas kernels for 6%

profile of v2, /device:TPU:1, one launch (start us, length us, event | category | flops | bytes accessed | tf_op | source)
XLA Modules:
  0.0 69.5 jit_solution(6200274745929997242)
XLA Ops:
  1.3 1.9 %shard_map.102.packed = bf16[208,512]{1,0:T(8,128)(2,1)} custom-call(bf16[1,192,256]{2,1,0:T(8,128)(2,1)} %keys.1, bf16[1,192,256]{2,1,0:T(8,128)(2,1)} %values.1, s32[1,192]{1,0:T(1,128)} %slot_pos.1, s32[1,1]{1,0:T(1,128)S(6)} %copy.11.counts, s32[336]{0:T(512)} %seg_id.1), custom_call_target="tpu_custom_call" | custom-call | tf_op jit(solution)/shard_map/pallas_call | solution.py:63
  3.1 5.5 %collective-permute-start.1 = (bf16[208,512]{1,0:T(8,128)(2,1)}, bf16[208,512]{1,0:T(8,128)(2,1)S(1)}, u32[]{:S(2)}, u32[]{:S(2)}) collective-permute-start(bf16[208,512]{1,0:T(8,128)(2,1)} %shard_map.102.packed), channel_id=1, source_target_pairs={{0,384},{384,0},{1,385},{385,1},{2,386},{386,2},{3,387},{387,3},{4... | collective-permute-start | bytes 638984 | tf_op jit(solution)/shard_map/ppermute | solution.py:276
  8.6 3.2 %collective-permute-start = (bf16[208,512]{1,0:T(8,128)(2,1)}, bf16[208,512]{1,0:T(8,128)(2,1)S(1)}, u32[]{:S(2)}, u32[]{:S(2)}) collective-permute-start(bf16[208,512]{1,0:T(8,128)(2,1)} %shard_map.102.packed), channel_id=1, source_target_pairs={{0,2},{1,3},{2,4},{3,5},{4,6},{5,7},{6,8},{7,9},{8,10},{9,11},{10,... | collective-permute-start | bytes 638984 | tf_op jit(solution)/shard_map/ppermute | solution.py:261
  11.9 0.2 collective-permute-done.1.refs_1_
  12.0 4.8 %collective-permute-start.3 = (bf16[208,512]{1,0:T(8,128)(2,1)S(1)}, bf16[208,512]{1,0:T(8,128)(2,1)S(1)}, u32[]{:S(2)}, u32[]{:S(2)}) collective-permute-start(bf16[208,512]{1,0:T(8,128)(2,1)S(1)} %collective-permute-done.1.refs_1_), channel_id=1, source_target_pairs={{0,2},{1,3},{2,4},{3,5},{4,6},{5,7},{6,8},{7,9},{8,10},{9,11},{10,... | collective-permute-start | bytes 638984 | tf_op jit(solution)/shard_map/ppermute | solution.py:261
  16.9 0.9 %copy-done = bf16[208,512]{1,0:T(8,128)(2,1)S(1)} copy-done((bf16[208,512]{1,0:T(8,128)(2,1)S(1)}, bf16[208,512]{1,0:T(8,128)(2,1)}, u32[]{:S(2)}) %copy-start) | copy-done | bytes 213016
  17.8 1.1 %copy-done.1 = bf16[1,192,1792]{2,1,0:T(8,128)(2,1)S(1)} copy-done((bf16[1,192,1792]{2,1,0:T(8,128)(2,1)S(1)}, bf16[1,192,1792]{2,1,0:T(8,128)(2,1)}, u32[]{:S(2)}) %copy-start.1) | copy-done | bytes 688152
  18.9 1.1 %copy-done.2 = bf16[1,192,1792]{2,1,0:T(8,128)(2,1)S(1)} copy-done((bf16[1,192,1792]{2,1,0:T(8,128)(2,1)S(1)}, bf16[1,192,1792]{2,1,0:T(8,128)(2,1)}, u32[]{:S(2)}) %copy-start.2) | copy-done | bytes 688152
  20.0 0.6 shard_map.103
  20.7 14.2 %collective-permute-start.2 = (bf16[208,512]{1,0:T(8,128)(2,1)S(1)}, bf16[208,512]{1,0:T(8,128)(2,1)S(1)}, u32[]{:S(2)}, u32[]{:S(2)}) collective-permute-start(bf16[208,512]{1,0:T(8,128)(2,1)S(1)} %broadcast_select_fusion.1), channel_id=1, source_target_pairs={{0,1},{1,0},{2,3},{3,2},{4,5},{5,4},{6,7},{7,6},{8,9},{9,8},{10,11... | collective-permute-start | bytes 638984 | tf_op jit(solution)/shard_map/ppermute | solution.py:281
  35.0 1.9 %collective-permute-start.4 = (bf16[208,512]{1,0:T(8,128)(2,1)S(1)}, bf16[208,512]{1,0:T(8,128)(2,1)S(1)}, u32[]{:S(2)}, u32[]{:S(2)}) collective-permute-start(bf16[208,512]{1,0:T(8,128)(2,1)S(1)} %broadcast_select_fusion), channel_id=1, source_target_pairs={{0,1},{1,0},{2,3},{3,2},{4,5},{5,4},{6,7},{7,6},{8,9},{9,8},{10,11... | collective-permute-start | bytes 638984 | tf_op jit(solution)/shard_map/ppermute | solution.py:281
  36.9 1.4 %collective-permute-done.4.refs_3_ = bf16[208,512]{1,0:T(8,128)(2,1)S(1)} collective-permute-done((bf16[208,512]{1,0:T(8,128)(2,1)S(1)}, bf16[208,512]{1,0:T(8,128)(2,1)S(1)}, u32[]{:S(2)}, u32[]{:S(2)}) %collective-permute-start.4) | collective-permute-done | bytes 213024 | tf_op jit(solution)/shard_map/ppermute | solution.py:281
  38.3 9.8 %shard_map.104 = (bf16[1,192,1792]{2,1,0:T(8,128)(2,1)}, bf16[14,192,1152]{2,1,0:T(8,128)(2,1)S(1)}, bf16[14,192,384]{2,1,0:T(8,128)(2,1)S(1)}, bf16[2,192,512]{...) custom-call(bf16[192,1792]{1,0:T(8,128)(2,1)S(1)} %get-tuple-element.17.queries, ...), custom_call_target="tpu_custom_call" | custom-call | flops 3500000000 | bytes 12000000 | tf_op jit(solution)/shard_map/pallas_call | solution.py:184
  48.2 2.2 %collective-permute-start.5 = (bf16[2,192,512]{2,1,0:T(8,128)(2,1)S(1)}, bf16[2,192,512]{2,1,0:T(8,128)(2,1)S(1)}, u32[]{:S(2)}, u32[]{:S(2)}) collective-permute-start(bf16[2,192,512]{2,1,0:T(8,128)(2,1)S(1)} %get-tuple-element.24), channel_id=1, source_target_pairs={{0,1},{1,0},{2,3},{3,2},{4,5},{5,4},{6,7},{7,6},{8,9},{9,8},{10,11... | collective-permute-start | bytes 1179656 | tf_op jit(solution)/shard_map/ppermute | solution.py:281
  50.4 1.2 %shard_map.106 = f32[2,192,512]{2,1,0:T(8,128)S(1)} custom-call(bf16[14,128,192]{2,1,0:T(8,128)(2,1)S(1)} %get-tuple-element.19.queries_t, bf16[14,128,192]{2,1,0:T(8,128)(2,1)S(1)} %get-tuple-element.20.grads_t, bf16[14,192,1152]{2,1,0:T(8,128)(2,1)S(1)} %get-tuple-element.26.dscores, bf16[14,192,384]{2,1,0:T(8,128)(2,1)S(1)} %get-tuple-element.28.probs), custom_call_target="tpu_custom_call" | custom-call | flops 530000000 | bytes 6000000 | tf_op jit(solution)/shard_map/pallas_call | solution.py:224
  51.8 0.2 fusion.2
  52.0 3.6 %collective-permute-start.7 = (bf16[192,512]{1,0:T(8,128)(2,1)S(1)}, bf16[192,512]{1,0:T(8,128)(2,1)S(1)}, u32[]{:S(2)}, u32[]{:S(2)}) collective-permute-start(bf16[192,512]{1,0:T(8,128)(2,1)S(1)} %fusion.3), channel_id=1, source_target_pairs={{0,384},{384,0},{1,385},{385,1},{2,386},{386,2},{3,387},{387,3},{4... | collective-permute-start | bytes 589832 | tf_op jit(solution)/shard_map/ppermute | solution.py:276
  55.7 1.3 %collective-permute-start.6 = (bf16[192,512]{1,0:T(8,128)(2,1)S(1)}, bf16[192,512]{1,0:T(8,128)(2,1)S(1)}, u32[]{:S(2)}, u32[]{:S(2)}) collective-permute-start(bf16[192,512]{1,0:T(8,128)(2,1)S(1)} %get-tuple-element.32), channel_id=1, source_target_pairs={{2,384},{3,385},{4,386},{5,387},{6,388},{7,389},{8,390},{9,391},{1... | collective-permute-start | bytes 589832 | tf_op jit(solution)/shard_map/ppermute | solution.py:272
  57.0 1.3 %collective-permute-start.8 = (bf16[192,512]{1,0:T(8,128)(2,1)S(1)}, bf16[192,512]{1,0:T(8,128)(2,1)S(1)}, u32[]{:S(2)}, u32[]{:S(2)}) collective-permute-start(bf16[192,512]{1,0:T(8,128)(2,1)S(1)} %get-tuple-element.33), channel_id=1, source_target_pairs={{2,0},{3,1},{4,2},{5,3},{6,4},{7,5},{8,6},{9,7},{10,8},{11,9},{12,... | collective-permute-start | bytes 589832 | tf_op jit(solution)/shard_map/ppermute | solution.py:261
  58.3 2.6 %shard_map.105 = bf16[1,192,1792]{2,1,0:T(8,128)(2,1)} custom-call(bf16[14,192,1152]{2,1,0:T(8,128)(2,1)S(1)} %get-tuple-element.26.dscores, bf16[2,1152,128]{2,1,0:T(8,128)(2,1)S(1)} %get-tuple-element.27.keys), custom_call_target="tpu_custom_call" | custom-call | flops 800000000 | bytes 8000000 | tf_op jit(solution)/shard_map/pallas_call | solution.py:244
  60.9 0.7 %collective-permute-done.7 = bf16[192,512]{1,0:T(8,128)(2,1)S(1)} collective-permute-done((bf16[192,512]{1,0:T(8,128)(2,1)S(1)}, bf16[192,512]{1,0:T(8,128)(2,1)S(1)}, u32[]{:S(2)}, u32[]{:S(2)}) %collective-permute-start.7) | collective-permute-done | bytes 196640 | tf_op jit(solution)/shard_map/ppermute | solution.py:276
  61.7 4.3 %collective-permute-done.6 = bf16[192,512]{1,0:T(8,128)(2,1)S(1)} collective-permute-done((bf16[192,512]{1,0:T(8,128)(2,1)S(1)}, bf16[192,512]{1,0:T(8,128)(2,1)S(1)}, u32[]{:S(2)}, u32[]{:S(2)}) %collective-permute-start.6) | collective-permute-done | bytes 196640 | tf_op jit(solution)/shard_map/ppermute | solution.py:272
  65.9 2.8 %collective-permute-done.8 = bf16[192,512]{1,0:T(8,128)(2,1)S(1)} collective-permute-done((bf16[192,512]{1,0:T(8,128)(2,1)S(1)}, bf16[192,512]{1,0:T(8,128)(2,1)S(1)}, u32[]{:S(2)}, u32[]{:S(2)}) %collective-permute-start.8) | collective-permute-done | bytes 196640 | tf_op jit(solution)/shard_map/ppermute | solution.py:261
  68.8 0.8 %fusion.11 = (bf16[1,192,256]{2,1,0:T(8,128)(2,1)}, bf16[1,192,256]{2,1,0:T(8,128)(2,1)}) fusion(f32[192,512]{1,0:T(8,128)S(1)} %slice_bitcast_fusion, bf16[192,512]{1,0:T(8,128)(2,1)S(1)} %collective-permute-done.8, bf16[192,512]{1,0:T(8,128)(2,1)S(1)} %collective-permute-done.7, bf16[192,512]{1,0:T(8,128)(2,1)S(1)} %collective-permute-done.6), kind=kLoop, calls=%fused_computation.21 | loop fusion | flops 688128 | bytes 1179648 | tf_op jit(solution)/shard_map/broadcast_in_dim | solution.py:307
  (12 shorter events, 0.3 us)
Async XLA Ops:
  3.1 8.9 %collective-permute-start.1 = (bf16[208,512]{1,0:T(8,128)(2,1)}, bf16[208,512]{1,0:T(8,128)(2,1)S(1)}, u32[]{:S(2)}, u32[]{:S(2)}) collective-permute-start(bf16[208,512]{1,0:T(8,128)(2,1)} %shard_map.102.packed), channel_id=1, source_target_pairs={{0,384},{384,0},{1,385},{385,1},{2,386},{386,2},{3,387},{387,3},{4... | collective-permute-start | bytes 638984 | tf_op jit(solution)/shard_map/ppermute | solution.py:276
  8.6 8.3 %collective-permute-start = (bf16[208,512]{1,0:T(8,128)(2,1)}, bf16[208,512]{1,0:T(8,128)(2,1)S(1)}, u32[]{:S(2)}, u32[]{:S(2)}) collective-permute-start(bf16[208,512]{1,0:T(8,128)(2,1)} %shard_map.102.packed), channel_id=1, source_target_pairs={{0,2},{1,3},{2,4},{3,5},{4,6},{5,7},{6,8},{7,9},{8,10},{9,11},{10,... | collective-permute-start | bytes 638984 | tf_op jit(solution)/shard_map/ppermute | solution.py:261
  12.0 22.9 %collective-permute-start.3 = (bf16[208,512]{1,0:T(8,128)(2,1)S(1)}, bf16[208,512]{1,0:T(8,128)(2,1)S(1)}, u32[]{:S(2)}, u32[]{:S(2)}) collective-permute-start(bf16[208,512]{1,0:T(8,128)(2,1)S(1)} %collective-permute-done.1.refs_1_), channel_id=1, source_target_pairs={{0,2},{1,3},{2,4},{3,5},{4,6},{5,7},{6,8},{7,9},{8,10},{9,11},{10,... | collective-permute-start | bytes 638984 | tf_op jit(solution)/shard_map/ppermute | solution.py:261
  16.9 0.9 %copy-start = (bf16[208,512]{1,0:T(8,128)(2,1)S(1)}, bf16[208,512]{1,0:T(8,128)(2,1)}, u32[]{:S(2)}) copy-start(bf16[208,512]{1,0:T(8,128)(2,1)} %shard_map.102.packed) | copy-start | bytes 638980
  17.8 1.1 %copy-start.1 = (bf16[1,192,1792]{2,1,0:T(8,128)(2,1)S(1)}, bf16[1,192,1792]{2,1,0:T(8,128)(2,1)}, u32[]{:S(2)}) copy-start(bf16[1,192,1792]{2,1,0:T(8,128)(2,1)} %queries.1) | copy-start | bytes 2064388
  18.9 1.1 %copy-start.2 = (bf16[1,192,1792]{2,1,0:T(8,128)(2,1)S(1)}, bf16[1,192,1792]{2,1,0:T(8,128)(2,1)}, u32[]{:S(2)}) copy-start(bf16[1,192,1792]{2,1,0:T(8,128)(2,1)} %grads.1) | copy-start | bytes 2064388
  20.7 16.2 %collective-permute-start.2 = (bf16[208,512]{1,0:T(8,128)(2,1)S(1)}, bf16[208,512]{1,0:T(8,128)(2,1)S(1)}, u32[]{:S(2)}, u32[]{:S(2)}) collective-permute-start(bf16[208,512]{1,0:T(8,128)(2,1)S(1)} %broadcast_select_fusion.1), channel_id=1, source_target_pairs={{0,1},{1,0},{2,3},{3,2},{4,5},{5,4},{6,7},{7,6},{8,9},{9,8},{10,11... | collective-permute-start | bytes 638984 | tf_op jit(solution)/shard_map/ppermute | solution.py:281
  35.0 3.4 %collective-permute-start.4 = (bf16[208,512]{1,0:T(8,128)(2,1)S(1)}, bf16[208,512]{1,0:T(8,128)(2,1)S(1)}, u32[]{:S(2)}, u32[]{:S(2)}) collective-permute-start(bf16[208,512]{1,0:T(8,128)(2,1)S(1)} %broadcast_select_fusion), channel_id=1, source_target_pairs={{0,1},{1,0},{2,3},{3,2},{4,5},{5,4},{6,7},{7,6},{8,9},{9,8},{10,11... | collective-permute-start | bytes 638984 | tf_op jit(solution)/shard_map/ppermute | solution.py:281
  48.2 3.6 %collective-permute-start.5 = (bf16[2,192,512]{2,1,0:T(8,128)(2,1)S(1)}, bf16[2,192,512]{2,1,0:T(8,128)(2,1)S(1)}, u32[]{:S(2)}, u32[]{:S(2)}) collective-permute-start(bf16[2,192,512]{2,1,0:T(8,128)(2,1)S(1)} %get-tuple-element.24), channel_id=1, source_target_pairs={{0,1},{1,0},{2,3},{3,2},{4,5},{5,4},{6,7},{7,6},{8,9},{9,8},{10,11... | collective-permute-start | bytes 1179656 | tf_op jit(solution)/shard_map/ppermute | solution.py:281
  52.0 9.7 %collective-permute-start.7 = (bf16[192,512]{1,0:T(8,128)(2,1)S(1)}, bf16[192,512]{1,0:T(8,128)(2,1)S(1)}, u32[]{:S(2)}, u32[]{:S(2)}) collective-permute-start(bf16[192,512]{1,0:T(8,128)(2,1)S(1)} %fusion.3), channel_id=1, source_target_pairs={{0,384},{384,0},{1,385},{385,1},{2,386},{386,2},{3,387},{387,3},{4... | collective-permute-start | bytes 589832 | tf_op jit(solution)/shard_map/ppermute | solution.py:276
  55.7 10.2 %collective-permute-start.6 = (bf16[192,512]{1,0:T(8,128)(2,1)S(1)}, bf16[192,512]{1,0:T(8,128)(2,1)S(1)}, u32[]{:S(2)}, u32[]{:S(2)}) collective-permute-start(bf16[192,512]{1,0:T(8,128)(2,1)S(1)} %get-tuple-element.32), channel_id=1, source_target_pairs={{2,384},{3,385},{4,386},{5,387},{6,388},{7,389},{8,390},{9,391},{1... | collective-permute-start | bytes 589832 | tf_op jit(solution)/shard_map/ppermute | solution.py:272
  57.0 11.8 %collective-permute-start.8 = (bf16[192,512]{1,0:T(8,128)(2,1)S(1)}, bf16[192,512]{1,0:T(8,128)(2,1)S(1)}, u32[]{:S(2)}, u32[]{:S(2)}) collective-permute-start(bf16[192,512]{1,0:T(8,128)(2,1)S(1)} %get-tuple-element.33), channel_id=1, source_target_pairs={{2,0},{3,1},{4,2},{5,3},{6,4},{7,5},{8,6},{9,7},{10,8},{11,9},{12,... | collective-permute-start | bytes 589832 | tf_op jit(solution)/shard_map/ppermute | solution.py:261

commit v3 on v2

--- a/solution.py
+++ b/solution.py
@@ -235,20 +235,21 @@
     )(queries_t, grads_t, dscores, probs)
 
 
-def query_kernel(dscores, keys, grad_queries):
+def query_kernel(dscores, keys, attended, grad_queries, attended_out):
+    attended_out[...] = attended[...]
     for n in range(SHARING * KEY_HEADS):
         grad_queries[0, :, column(n)] = (nn(dscores[n], keys[n // SHARING]) * SCALE).astype(BF16)
 
 
-def query_gradients(dscores, keys):
+def query_gradients(dscores, keys, attended):
     return pl.pallas_call(
         query_kernel,
-        out_shape=jax.ShapeDtypeStruct((1, TOKENS, SHARING * KEY_HEADS * HEAD), BF16),
-        in_specs=[VMEM] * 2,
-        out_specs=VMEM,
+        out_shape=[jax.ShapeDtypeStruct((1, TOKENS, SHARING * KEY_HEADS * HEAD), BF16)] * 2,
+        in_specs=[VMEM] * 3,
+        out_specs=[VMEM] * 2,
         compiler_params=pltpu.CompilerParams(vmem_limit_bytes=24 * 2**20),
         cost_estimate=pl.CostEstimate(flops=800_000_000, bytes_accessed=8_000_000, transcendentals=0),
-    )(dscores, keys)
+    )(dscores, keys, attended)
 
 
 BLOCKS = ("seq", "tp")
@@ -284,13 +285,13 @@
 def body(queries, keys, values, grad_out, slot_pos, counts, seg_id):
     core = lax.axis_index(BLOCKS) % 2
     packed = pack(keys, values, slot_pos, counts, seg_id)
+    across = shift_across(packed, 2)
     other = exchange(packed)
     behind = shift_blocks(packed, 2)
-    across = shift_blocks(other, 2)
-    *turned, own = turn(queries, grad_out, packed, behind)
-    early = swap_cores(jnp.where(core == 0, own, behind))
-    late = swap_cores(jnp.where(core == 0, other, across))
-    pieces = (own, other, early, late, behind, across)
+    *turned, own = turn(queries, grad_out, packed, packed)
+    late = swap_cores(jnp.where(core == 0, other, behind))
+    early = swap_cores(jnp.where(core == 0, own, across))
+    pieces = (own, other, early, late, across, behind)
     attended, dscores, near_probs, middle, far, keys = attention(*turned, pieces)
     back = swap_cores(middle)
     near = near_gradients(turned[2], turned[3], dscores, near_probs)
@@ -298,10 +299,10 @@
     far = (far + jnp.where(core == 0, 0.0, back)).astype(BF16)
     near = near + jnp.where(core == 0, back, 0.0)
     far, dscores = lax.optimization_barrier((far, dscores))
-    from_across = shift_across(far[1], -2)
+    from_ahead = shift_blocks(far[1], -2)
+    from_across = shift_across(far[0], -2)
     from_other = exchange(near[1].astype(BF16))
-    from_ahead = shift_blocks(far[0], -2)
-    grad_queries = query_gradients(dscores, keys)
+    grad_queries, attended = query_gradients(dscores, keys, attended)
     half = KEY_HEADS * HEAD
     totals = [
         (near[0][:, at] + from_across[:, at].astype(F32) + from_other[:, at].astype(F32) + from_ahead[:, at].astype(F32))

time: 70 us -> 63.9 us (0.913)
  the two profiles are of different devices: /device:TPU:1 before, /device:TPU:250 now
where the time goes in v3:
time: 63.9 us; the launch traced here: 63.4 us
  starting transfers between devices  27.9 us (44%)
  Pallas kernels  16.1 us (25%)
  waiting for transfers between devices  13.7 us (21%)
  local copies, waits for them, and re-layouts  3.22 us (5%)
  between operations  1.48 us (2%)
  other arithmetic  1.04 us (2%)
    ppermute x2, starting transfers between devices, exchange(): return lax.ppermute(array, 'grp', [(0, 1), (1, 0)])  10.1 us
    pallas_call x1, Pallas kernels, attention(): pl.pallas_call(attention_kernel, out_shape=[jax.ShapeDtypeStruct((1, TOKE...  9.56 us
    ppermute x2, waiting for transfers between devices, shift_across(): return lax.ppermute(array, ALL, route)  7.18 us
    ppermute x3, starting transfers between devices, swap_cores(): return lax.ppermute(array, BLOCKS, [(i, i ^ 1) for i in range(count)])  6.79 us
    ppermute x2, starting transfers between devices, shift_blocks(): return lax.ppermute(array, BLOCKS, route)  6.57 us
    ppermute x2, starting transfers between devices, shift_across(): return lax.ppermute(array, ALL, route)  4.45 us
    unnamed x6, local copies, waits for them, and re-layouts  3.14 us
    pallas_call x1, Pallas kernels, query_gradients(): pl.pallas_call(query_kernel, out_shape=[jax.ShapeDtypeStruct((1, TOKENS,...  2.81 us
  transfers between devices with their start and end apart: 9, of which 4 were waited for; matrix products, arithmetic and copies ran while one was open for 0% of the time, Pallas kernels for 7%

profile of v3, /device:TPU:250, one launch (start us, length us, event | category | flops | bytes accessed | tf_op | source)
XLA Modules:
  0.0 63.4 jit_solution(15238850530174133430)
XLA Ops:
  1.3 1.9 %shard_map.102.packed.after = bf16[208,512]{1,0:T(8,128)(2,1)} custom-call(bf16[1,192,256]{2,1,0:T(8,128)(2,1)} %keys.1, bf16[1,192,256]{2,1,0:T(8,128)(2,1)} %values.1, s32[1,192]{1,0:T(1,128)} %slot_pos.1, s32[1,1]{1,0:T(1,128)S(6)} %copy.11.counts, s32[336]{0:T(512)} %seg_id.1), custom_call_target="tpu_custom_call" | custom-call | tf_op jit(solution)/shard_map/pallas_call | solution.py:63
  3.1 4.7 %collective-permute-start.3 = (bf16[208,512]{1,0:T(8,128)(2,1)}, bf16[208,512]{1,0:T(8,128)(2,1)S(1)}, u32[]{:S(2)}, u32[]{:S(2)}) collective-permute-start(bf16[208,512]{1,0:T(8,128)(2,1)} %shard_map.102.packed.after), channel_id=1, source_target_pairs={{0,2},{1,3},{2,4},{3,5},{4,6},{5,7},{6,8},{7,9},{8,10},{9,11},{10,... | collective-permute-start | bytes 638984 | tf_op jit(solution)/shard_map/ppermute | solution.py:262
  7.8 4.3 %collective-permute-start = (bf16[208,512]{1,0:T(8,128)(2,1)}, bf16[208,512]{1,0:T(8,128)(2,1)S(1)}, u32[]{:S(2)}, u32[]{:S(2)}) collective-permute-start(bf16[208,512]{1,0:T(8,128)(2,1)} %shard_map.102.packed.after), channel_id=1, source_target_pairs={{0,384},{384,0},{1,385},{385,1},{2,386},{386,2},{3,387},{387,3},{4... | collective-permute-start | bytes 638984 | tf_op jit(solution)/shard_map/ppermute | solution.py:277
  12.1 2.5 %collective-permute-start.1 = (bf16[208,512]{1,0:T(8,128)(2,1)}, bf16[208,512]{1,0:T(8,128)(2,1)S(1)}, u32[]{:S(2)}, u32[]{:S(2)}) collective-permute-start(bf16[208,512]{1,0:T(8,128)(2,1)} %shard_map.102.packed.after), channel_id=1, source_target_pairs={{0,386},{1,387},{2,388},{3,389},{4,390},{5,391},{6,392},{7,393},{8... | collective-permute-start | bytes 638984 | tf_op jit(solution)/shard_map/ppermute | solution.py:273
  14.7 0.0 copy-start
  14.7 0.9 %copy-done = bf16[208,512]{1,0:T(8,128)(2,1)S(1)} copy-done((bf16[208,512]{1,0:T(8,128)(2,1)S(1)}, bf16[208,512]{1,0:T(8,128)(2,1)}, u32[]{:S(2)}) %copy-start) | copy-done | bytes 213016
  15.6 1.1 %copy-done.1 = bf16[1,192,1792]{2,1,0:T(8,128)(2,1)S(1)} copy-done((bf16[1,192,1792]{2,1,0:T(8,128)(2,1)S(1)}, bf16[1,192,1792]{2,1,0:T(8,128)(2,1)}, u32[]{:S(2)}) %copy-start.1) | copy-done | bytes 688152
  16.7 1.1 %copy-done.2 = bf16[1,192,1792]{2,1,0:T(8,128)(2,1)S(1)} copy-done((bf16[1,192,1792]{2,1,0:T(8,128)(2,1)S(1)}, bf16[1,192,1792]{2,1,0:T(8,128)(2,1)}, u32[]{:S(2)}) %copy-start.2) | copy-done | bytes 688152
  17.8 0.6 shard_map.103
  18.5 2.8 %collective-permute-done.refs_1_ = bf16[208,512]{1,0:T(8,128)(2,1)S(1)} collective-permute-done((bf16[208,512]{1,0:T(8,128)(2,1)}, bf16[208,512]{1,0:T(8,128)(2,1)S(1)}, u32[]{:S(2)}, u32[]{:S(2)}) %collective-permute-start) | collective-permute-done | bytes 213024 | tf_op jit(solution)/shard_map/ppermute | solution.py:277
  21.2 1.9 %collective-permute-start.4 = (bf16[208,512]{1,0:T(8,128)(2,1)S(1)}, bf16[208,512]{1,0:T(8,128)(2,1)S(1)}, u32[]{:S(2)}, u32[]{:S(2)}) collective-permute-start(bf16[208,512]{1,0:T(8,128)(2,1)S(1)} %broadcast_select_fusion), channel_id=1, source_target_pairs={{0,1},{1,0},{2,3},{3,2},{4,5},{5,4},{6,7},{7,6},{8,9},{9,8},{10,11... | collective-permute-start | bytes 638984 | tf_op jit(solution)/shard_map/ppermute | solution.py:282
  23.2 2.4 %collective-permute-start.2 = (bf16[208,512]{1,0:T(8,128)(2,1)S(1)}, bf16[208,512]{1,0:T(8,128)(2,1)S(1)}, u32[]{:S(2)}, u32[]{:S(2)}) collective-permute-start(bf16[208,512]{1,0:T(8,128)(2,1)S(1)} %broadcast_select_fusion.1), channel_id=1, source_target_pairs={{0,1},{1,0},{2,3},{3,2},{4,5},{5,4},{6,7},{7,6},{8,9},{9,8},{10,11... | collective-permute-start | bytes 638984 | tf_op jit(solution)/shard_map/ppermute | solution.py:282
  25.6 1.1 %collective-permute-done.2.refs_2_ = bf16[208,512]{1,0:T(8,128)(2,1)S(1)} collective-permute-done((bf16[208,512]{1,0:T(8,128)(2,1)S(1)}, bf16[208,512]{1,0:T(8,128)(2,1)S(1)}, u32[]{:S(2)}, u32[]{:S(2)}) %collective-permute-start.2) | collective-permute-done | bytes 213024 | tf_op jit(solution)/shard_map/ppermute | solution.py:282
  26.7 9.6 %shard_map.104 = (bf16[1,192,1792]{2,1,0:T(8,128)(2,1)S(1)}, bf16[14,192,1152]{2,1,0:T(8,128)(2,1)S(1)}, bf16[14,192,384]{2,1,0:T(8,128)(2,1)S(1)}, bf16[2,192,5...) custom-call(bf16[192,1792]{1,0:T(8,128)(2,1)S(1)} %get-tuple-element.19.queries, ...), custom_call_target="tpu_custom_call" | custom-call | flops 3500000000 | bytes 12000000 | tf_op jit(solution)/shard_map/pallas_call | solution.py:184
  36.3 2.5 %collective-permute-start.5 = (bf16[2,192,512]{2,1,0:T(8,128)(2,1)S(1)}, bf16[2,192,512]{2,1,0:T(8,128)(2,1)S(1)}, u32[]{:S(2)}, u32[]{:S(2)}) collective-permute-start(bf16[2,192,512]{2,1,0:T(8,128)(2,1)S(1)} %get-tuple-element.25), channel_id=1, source_target_pairs={{0,1},{1,0},{2,3},{3,2},{4,5},{5,4},{6,7},{7,6},{8,9},{9,8},{10,11... | collective-permute-start | bytes 1179656 | tf_op jit(solution)/shard_map/ppermute | solution.py:282
  38.7 1.2 %shard_map.106 = f32[2,192,512]{2,1,0:T(8,128)S(1)} custom-call(bf16[14,128,192]{2,1,0:T(8,128)(2,1)S(1)} %get-tuple-element.21.queries_t, bf16[14,128,192]{2,1,0:T(8,128)(2,1)S(1)} %get-tuple-element.22.grads_t, bf16[14,192,1152]{2,1,0:T(8,128)(2,1)S(1)} %get-tuple-element.27.dscores, bf16[14,192,384]{2,1,0:T(8,128)(2,1)S(1)} %get-tuple-element.32.probs), custom_call_target="tpu_custom_call" | custom-call | flops 530000000 | bytes 6000000 | tf_op jit(solution)/shard_map/pallas_call | solution.py:224
  40.0 0.2 fusion.2
  40.2 5.8 %collective-permute-start.7 = (bf16[192,512]{1,0:T(8,128)(2,1)S(1)}, bf16[192,512]{1,0:T(8,128)(2,1)S(1)}, u32[]{:S(2)}, u32[]{:S(2)}) collective-permute-start(bf16[192,512]{1,0:T(8,128)(2,1)S(1)} %fusion.3), channel_id=1, source_target_pairs={{0,384},{384,0},{1,385},{385,1},{2,386},{386,2},{3,387},{387,3},{4... | collective-permute-start | bytes 589832 | tf_op jit(solution)/shard_map/ppermute | solution.py:277
  46.1 1.9 %collective-permute-start.6 = (bf16[192,512]{1,0:T(8,128)(2,1)S(1)}, bf16[192,512]{1,0:T(8,128)(2,1)S(1)}, u32[]{:S(2)}, u32[]{:S(2)}) collective-permute-start(bf16[192,512]{1,0:T(8,128)(2,1)S(1)} %get-tuple-element.36), channel_id=1, source_target_pairs={{2,384},{3,385},{4,386},{5,387},{6,388},{7,389},{8,390},{9,391},{1... | collective-permute-start | bytes 589832 | tf_op jit(solution)/shard_map/ppermute | solution.py:273
  48.0 1.9 %collective-permute-start.8 = (bf16[192,512]{1,0:T(8,128)(2,1)S(1)}, bf16[192,512]{1,0:T(8,128)(2,1)S(1)}, u32[]{:S(2)}, u32[]{:S(2)}) collective-permute-start(bf16[192,512]{1,0:T(8,128)(2,1)S(1)} %get-tuple-element.37), channel_id=1, source_target_pairs={{2,0},{3,1},{4,2},{5,3},{6,4},{7,5},{8,6},{9,7},{10,8},{11,9},{12,... | collective-permute-start | bytes 589832 | tf_op jit(solution)/shard_map/ppermute | solution.py:262
  49.9 2.8 %shard_map.105 = (bf16[1,192,1792]{2,1,0:T(8,128)(2,1)}, bf16[1,192,1792]{2,1,0:T(8,128)(2,1)}) custom-call(bf16[14,192,1152]{2,1,0:T(8,128)(2,1)S(1)} %get-tuple-element.27.dscores, bf16[2,1152,128]{2,1,0:T(8,128)(2,1)S(1)} %get-tuple-element.28.keys, bf16[1,192,1792]{2,1,0:T(8,128)(2,1)S(1)} %get-tuple-element.29.attended), custom_call_target="tpu_custom_call" | custom-call | flops 800000000 | bytes 8000000 | tf_op jit(solution)/shard_map/pallas_call | solution.py:245
  52.8 7.2 %collective-permute-done.6 = bf16[192,512]{1,0:T(8,128)(2,1)S(1)} collective-permute-done((bf16[192,512]{1,0:T(8,128)(2,1)S(1)}, bf16[192,512]{1,0:T(8,128)(2,1)S(1)}, u32[]{:S(2)}, u32[]{:S(2)}) %collective-permute-start.6) | collective-permute-done | bytes 196640 | tf_op jit(solution)/shard_map/ppermute | solution.py:273
  60.0 2.7 %collective-permute-done.8 = bf16[192,512]{1,0:T(8,128)(2,1)S(1)} collective-permute-done((bf16[192,512]{1,0:T(8,128)(2,1)S(1)}, bf16[192,512]{1,0:T(8,128)(2,1)S(1)}, u32[]{:S(2)}, u32[]{:S(2)}) %collective-permute-start.8) | collective-permute-done | bytes 196640 | tf_op jit(solution)/shard_map/ppermute | solution.py:262
  62.6 0.8 %fusion.11 = (bf16[1,192,256]{2,1,0:T(8,128)(2,1)}, bf16[1,192,256]{2,1,0:T(8,128)(2,1)}) fusion(f32[192,512]{1,0:T(8,128)S(1)} %slice_bitcast_fusion, bf16[192,512]{1,0:T(8,128)(2,1)S(1)} %collective-permute-done.8, bf16[192,512]{1,0:T(8,128)(2,1)S(1)} %collective-permute-done.7, bf16[192,512]{1,0:T(8,128)(2,1)S(1)} %collective-permute-done.6), kind=kLoop, calls=%fused_computation.21 | loop fusion | flops 688128 | bytes 1179648 | tf_op jit(solution)/shard_map/broadcast_in_dim | solution.py:308
  (12 shorter events, 0.1 us)
Async XLA Ops:
  3.1 15.3 %collective-permute-start.3 = (bf16[208,512]{1,0:T(8,128)(2,1)}, bf16[208,512]{1,0:T(8,128)(2,1)S(1)}, u32[]{:S(2)}, u32[]{:S(2)}) collective-permute-start(bf16[208,512]{1,0:T(8,128)(2,1)} %shard_map.102.packed.after), channel_id=1, source_target_pairs={{0,2},{1,3},{2,4},{3,5},{4,6},{5,7},{6,8},{7,9},{8,10},{9,11},{10,... | collective-permute-start | bytes 638984 | tf_op jit(solution)/shard_map/ppermute | solution.py:262
  7.8 13.4 %collective-permute-start = (bf16[208,512]{1,0:T(8,128)(2,1)}, bf16[208,512]{1,0:T(8,128)(2,1)S(1)}, u32[]{:S(2)}, u32[]{:S(2)}) collective-permute-start(bf16[208,512]{1,0:T(8,128)(2,1)} %shard_map.102.packed.after), channel_id=1, source_target_pairs={{0,384},{384,0},{1,385},{385,1},{2,386},{386,2},{3,387},{387,3},{4... | collective-permute-start | bytes 638984 | tf_op jit(solution)/shard_map/ppermute | solution.py:277
  12.1 11.0 %collective-permute-start.1 = (bf16[208,512]{1,0:T(8,128)(2,1)}, bf16[208,512]{1,0:T(8,128)(2,1)S(1)}, u32[]{:S(2)}, u32[]{:S(2)}) collective-permute-start(bf16[208,512]{1,0:T(8,128)(2,1)} %shard_map.102.packed.after), channel_id=1, source_target_pairs={{0,386},{1,387},{2,388},{3,389},{4,390},{5,391},{6,392},{7,393},{8... | collective-permute-start | bytes 638984 | tf_op jit(solution)/shard_map/ppermute | solution.py:273
  14.7 1.0 %copy-start = (bf16[208,512]{1,0:T(8,128)(2,1)S(1)}, bf16[208,512]{1,0:T(8,128)(2,1)}, u32[]{:S(2)}) copy-start(bf16[208,512]{1,0:T(8,128)(2,1)} %shard_map.102.packed.after) | copy-start | bytes 638980
  15.6 1.1 %copy-start.1 = (bf16[1,192,1792]{2,1,0:T(8,128)(2,1)S(1)}, bf16[1,192,1792]{2,1,0:T(8,128)(2,1)}, u32[]{:S(2)}) copy-start(bf16[1,192,1792]{2,1,0:T(8,128)(2,1)} %queries.1) | copy-start | bytes 2064388
  16.7 1.1 %copy-start.2 = (bf16[1,192,1792]{2,1,0:T(8,128)(2,1)S(1)}, bf16[1,192,1792]{2,1,0:T(8,128)(2,1)}, u32[]{:S(2)}) copy-start(bf16[1,192,1792]{2,1,0:T(8,128)(2,1)} %grads.1) | copy-start | bytes 2064388
  21.2 4.4 %collective-permute-start.4 = (bf16[208,512]{1,0:T(8,128)(2,1)S(1)}, bf16[208,512]{1,0:T(8,128)(2,1)S(1)}, u32[]{:S(2)}, u32[]{:S(2)}) collective-permute-start(bf16[208,512]{1,0:T(8,128)(2,1)S(1)} %broadcast_select_fusion), channel_id=1, source_target_pairs={{0,1},{1,0},{2,3},{3,2},{4,5},{5,4},{6,7},{7,6},{8,9},{9,8},{10,11... | collective-permute-start | bytes 638984 | tf_op jit(solution)/shard_map/ppermute | solution.py:282
  23.2 3.5 %collective-permute-start.2 = (bf16[208,512]{1,0:T(8,128)(2,1)S(1)}, bf16[208,512]{1,0:T(8,128)(2,1)S(1)}, u32[]{:S(2)}, u32[]{:S(2)}) collective-permute-start(bf16[208,512]{1,0:T(8,128)(2,1)S(1)} %broadcast_select_fusion.1), channel_id=1, source_target_pairs={{0,1},{1,0},{2,3},{3,2},{4,5},{5,4},{6,7},{7,6},{8,9},{9,8},{10,11... | collective-permute-start | bytes 638984 | tf_op jit(solution)/shard_map/ppermute | solution.py:282
  36.3 3.7 %collective-permute-start.5 = (bf16[2,192,512]{2,1,0:T(8,128)(2,1)S(1)}, bf16[2,192,512]{2,1,0:T(8,128)(2,1)S(1)}, u32[]{:S(2)}, u32[]{:S(2)}) collective-permute-start(bf16[2,192,512]{2,1,0:T(8,128)(2,1)S(1)} %get-tuple-element.25), channel_id=1, source_target_pairs={{0,1},{1,0},{2,3},{3,2},{4,5},{5,4},{6,7},{7,6},{8,9},{9,8},{10,11... | collective-permute-start | bytes 1179656 | tf_op jit(solution)/shard_map/ppermute | solution.py:282
  40.2 12.5 %collective-permute-start.7 = (bf16[192,512]{1,0:T(8,128)(2,1)S(1)}, bf16[192,512]{1,0:T(8,128)(2,1)S(1)}, u32[]{:S(2)}, u32[]{:S(2)}) collective-permute-start(bf16[192,512]{1,0:T(8,128)(2,1)S(1)} %fusion.3), channel_id=1, source_target_pairs={{0,384},{384,0},{1,385},{385,1},{2,386},{386,2},{3,387},{387,3},{4... | collective-permute-start | bytes 589832 | tf_op jit(solution)/shard_map/ppermute | solution.py:277
  46.1 13.9 %collective-permute-start.6 = (bf16[192,512]{1,0:T(8,128)(2,1)S(1)}, bf16[192,512]{1,0:T(8,128)(2,1)S(1)}, u32[]{:S(2)}, u32[]{:S(2)}) collective-permute-start(bf16[192,512]{1,0:T(8,128)(2,1)S(1)} %get-tuple-element.36), channel_id=1, source_target_pairs={{2,384},{3,385},{4,386},{5,387},{6,388},{7,389},{8,390},{9,391},{1... | collective-permute-start | bytes 589832 | tf_op jit(solution)/shard_map/ppermute | solution.py:273
  48.0 14.6 %collective-permute-start.8 = (bf16[192,512]{1,0:T(8,128)(2,1)S(1)}, bf16[192,512]{1,0:T(8,128)(2,1)S(1)}, u32[]{:S(2)}, u32[]{:S(2)}) collective-permute-start(bf16[192,512]{1,0:T(8,128)(2,1)S(1)} %get-tuple-element.37), channel_id=1, source_target_pairs={{2,0},{3,1},{4,2},{5,3},{6,4},{7,5},{8,6},{9,7},{10,8},{11,9},{12,... | collective-permute-start | bytes 589832 | tf_op jit(solution)/shard_map/ppermute | solution.py:262
